TPU v7x, 256 devices: a whole 4x4x8 slice. The times are simulated.
256 devices in a mesh: lon: 32 (over y_lo, z, core), lat: 8 (over y_hi, x).
Axes of the slice: x: 4, y: 4 (y_hi: 2, y_lo: 2; y = y_hi * 2 + y_lo), z: 8, core: 2. Of those that a mesh axis runs over, the one named last changes fastest.
Arguments:
- field: bfloat16 [512, 128, 512], P('lon', 'lat'), may hold values from -6 to 6
- cotangent: bfloat16 [512, 128, 512], P('lon', 'lat'), may hold values from -6 to 6
- land_sea: int32 [512, 128], P('lon', 'lat'), may hold values 0 or 1
- fold_partner: int32 [512], replicated, may hold values from 0 to 511, as said below
- depth_kernel: float32 [49, 512], replicated, may hold values from -0.875 to 0.875
- norm_gain: float32 [512], replicated, may hold values from 0.5 to 1.5
- w_up: bfloat16 [512, 2048], replicated, may hold values from -0.25 to 0.25
- b_up: float32 [2048], replicated, may hold values from -3 to 3
- w_down: bfloat16 [2048, 512], replicated, may hold values from -0.125 to 0.125
Outputs:
- grad_field: bfloat16 [512, 128, 512], P('lon', 'lat')
- grad_up: float32 [512, 2048], P(('lon', 'lat'))
- grad_down: float32 [2048, 512], P(('lon', 'lat'))
- grad_kernel: float32 [49, 512], replicated
- grad_gain: float32 [512], replicated
- grad_bias: float32 [2048], replicated
Inputs may be any that keep to these rules, and one draw needn't show every extreme that they name: fold_partner[j] = (fold_partner[0] - j) mod 512 for every column j, a mirror of the columns; 511 - fold_partner[0] is at least 16 and not a multiple of 16.
All inputs are finite; a program needn't handle non-finite values. No bound on the sum of `land_sea` on one device may be relied on, other than what follows from the above.
Results may differ from a plain program's by a relative error of at most 0.013.
Values may be sent and summed in bfloat16 or wider, within the bound.
No kernel may reach another device: no remote copies, remote signals or barrier semaphores. Data moves between devices by JAX's collectives and lax.ppermute only.
A program may use at most 128 MiB of HBM per device.

v0:
```python
import jax
import jax.numpy as jnp
from jax import lax
from jax.experimental import pallas as pl
from jax.experimental.pallas import tpu as pltpu
from jax.sharding import PartitionSpec as P

DEVICES = ("lon", "lat")
X_MASKS = (1, 2, 3)
Y_MASKS = (128, 4, 132)
Z_MASKS = (16, 32, 48, 96)
CORE_MASK = 8


def send(value, mask):
    return lax.ppermute(value, DEVICES, [(i, i ^ mask) for i in range(256)])


def to_next(value):
    return lax.ppermute(value, "lon", [(i, (i + 1) % 32) for i in range(32)])


def to_previous(value):
    return lax.ppermute(value, "lon", [((i + 1) % 32, i) for i in range(32)])


def to_north(value):
    return lax.ppermute(value, "lat", [(i, i + 1) for i in range(7)])


def to_south(value):
    return lax.ppermute(value, "lat", [(i + 1, i) for i in range(7)])


def top_to_next(value):
    pairs = [(i * 8 + 7, (i + 1) % 32 * 8 + 7) for i in range(32)]
    return lax.ppermute(value, DEVICES, pairs)


def top_to_previous(value):
    pairs = [((i + 1) % 32 * 8 + 7, i * 8 + 7) for i in range(32)]
    return lax.ppermute(value, DEVICES, pairs)


def mirror_tiles(value, half_turn, others, transfer):
    def branch(k):
        pairs = [(e * 8 + 7, ((2 * k - e) % 32) * 8 + 7) for e in range(32)]
        return lambda v, *rest: (lax.ppermute(v, DEVICES, pairs), *transfer(*rest))

    return lax.switch(half_turn, [branch(k) for k in range(16)], value, *others)


ROOT_2_PI = 0.7978845608028654
CUBIC = 0.044715
F32 = jnp.float32
BF16 = jnp.bfloat16


def spread_rows(ext_ref, wide, shifted):
    wide[...] = ext_ref[...].astype(F32)
    for b in range(7):
        shifted[b] = wide[:, b : b + 16, :]


def forward_kernel(
    at_ref, ext_ref, kern_ref, gain_ref, b_up_ref, d_out_ref, order_hbm, w_up_hbm, d_act_hbm,
    d_cells_hbm, half_ref, own_hbm, keep_hbm, send_hbm,
    wide, shifted, normed, ordered, upper, active, tile, mixed_ref, order_ref, w_up_ref, d_act_ref,
    d_upper_ref, own, keep, give, small_ref, d_cells, sems,
):
    core, x_at, y_at = at_ref[0], at_ref[1], at_ref[2]
    loads = [
        pltpu.make_async_copy(order_hbm, order_ref, sems.at[0]),
        pltpu.make_async_copy(w_up_hbm, w_up_ref, sems.at[1]),
        pltpu.make_async_copy(d_act_hbm, d_act_ref, sems.at[2]),
    ]
    for load in loads:
        load.start()
    spread_rows(ext_ref, wide, shifted)

    def conv_step(step, carry):
        lanes = pl.ds(pl.multiple_of(step * 128, 128), 128)
        totals = [jnp.zeros((16, 128), F32)] * 16
        for b in range(7):
            weights = [kern_ref[a * 7 + b : a * 7 + b + 1, lanes] for a in range(7)]
            for r in range(22):
                cells = shifted[b, r, :, lanes]
                for a in range(max(0, r - 15), min(7, r + 1)):
                    totals[r - a] = totals[r - a] + cells * weights[a]
        for x in range(16):
            mixed_ref[x * 16 : x * 16 + 16, lanes] = totals[x]
        return carry

    lax.fori_loop(0, 4, conv_step, 0)

    def norm_step(step, carry):
        rows = pl.ds(pl.multiple_of(step * 32, 32), 32)
        cells = mixed_ref[rows, :]
        center = cells - jnp.mean(cells, axis=-1, keepdims=True)
        spread = jnp.mean(center * center, axis=-1, keepdims=True)
        normed[rows, :] = (center * lax.rsqrt(spread + 1e-6) * gain_ref[...]).astype(BF16)
        return carry

    lax.fori_loop(0, 8, norm_step, 0)
    for load in loads:
        load.wait()
    ordered[...] = jnp.dot(normed[...], order_ref[...], preferred_element_type=F32).astype(BF16)

    for t in range(4):
        lanes = slice(t * 512, t * 512 + 512)
        upper[...] = jnp.dot(normed[...], w_up_ref[:, lanes], preferred_element_type=F32)

        def gelu_step(step, bias):
            rows = pl.ds(pl.multiple_of(step * 32, 32), 32)
            u = upper[rows, :] + b_up_ref[:, lanes]
            square = u * u
            th = jnp.tanh(ROOT_2_PI * (u + CUBIC * (square * u)))
            half = 0.5 * (1.0 + th)
            active[rows, :] = (u * half).astype(BF16)
            slope = half + (0.5 * ROOT_2_PI) * u * (1.0 - th * th) * (1.0 + (3.0 * CUBIC) * square)
            d_up = (d_act_ref[rows, lanes] * slope).astype(BF16)
            d_upper_ref[rows, lanes] = d_up
            return bias + jnp.sum(d_up.astype(F32), axis=0, keepdims=True)

        small_ref[50 + t : 51 + t, :] = lax.fori_loop(0, 8, gelu_step, jnp.zeros((1, 512), F32))
        tile[...] = lax.dot_general(
            active[...], d_out_ref[...], (((0,), (0,)), ((), ())), preferred_element_type=F32
        )
        for y_hi in range(2):
            k_y = (y_hi * 2 + t // 2) ^ y_at
            for k_x in range(4):
                base = y_hi * 32 + (k_x ^ x_at) * 8
                for mine in range(2):
                    at = base + ((1 - core) if mine == 0 else core) * 64
                    piece = jnp.concatenate(
                        [tile[pl.ds(pl.multiple_of(at + zz * 128, 8), 8), :] for zz in range(4)],
                        axis=0,
                    )
                    at = k_y * 64 + (t % 2) * 32
                    rows = pl.ds(pl.multiple_of(at, 32), 32)
                    if mine == 0:
                        give[pl.ds(pl.multiple_of(k_x * 512 + at, 32), 32), :] = piece.astype(BF16)
                    elif k_x == 0:
                        own[rows, :] = piece
                    else:
                        keep[k_x - 1, rows, :] = piece.astype(BF16)

    for t in range(4):
        lanes = slice(t * 512, t * 512 + 512)
        tile[...] = lax.dot_general(
            ordered[...], d_upper_ref[:, lanes], (((0,), (0,)), ((), ())),
            preferred_element_type=F32,
        )
        at = 256 + t * 64
        own[at : at + 64, :] = tile[0:64, :]
        for k in range(4):
            piece = tile[256 + k * 64 : 320 + k * 64, :]
            give[k * 512 + at : k * 512 + at + 64, :] = piece.astype(BF16)
            if k:
                keep[k - 1, at : at + 64, :] = tile[k * 64 : k * 64 + 64, :].astype(BF16)
    stores = [
        pltpu.make_async_copy(give.at[0:2048], send_hbm.at[0:2048], sems.at[3]),
        pltpu.make_async_copy(keep, keep_hbm, sems.at[4]),
        pltpu.make_async_copy(own, own_hbm, sems.at[5]),
    ]
    for store in stores:
        store.start()
    upper[...] = lax.dot_general(
        d_upper_ref[...], w_up_ref[...], (((1,), (1,)), ((), ())), preferred_element_type=F32
    )

    def norm_step(step, gain_sum):
        rows = pl.ds(pl.multiple_of(step * 32, 32), 32)
        cells = mixed_ref[rows, :]
        center = cells - jnp.mean(cells, axis=-1, keepdims=True)
        spread = jnp.mean(center * center, axis=-1, keepdims=True)
        inverse = lax.rsqrt(spread + 1e-6)
        unit = center * inverse
        d = upper[rows, :]
        d_unit = d * gain_ref[...]
        along = jnp.mean(d_unit * unit, axis=-1, keepdims=True)
        d_center = (d_unit - unit * along) * inverse
        d_mixed = d_center - jnp.mean(d_center, axis=-1, keepdims=True)
        d_cells[pl.ds(step * 2, 2)] = d_mixed.reshape(2, 16, 512)
        return gain_sum + jnp.sum(d * unit, axis=0, keepdims=True)

    small_ref[49:50, :] = lax.fori_loop(0, 8, norm_step, jnp.zeros((1, 512), F32))
    small_ref[54:64, :] = jnp.zeros((10, 512), F32)
    stores.append(pltpu.make_async_copy(d_cells, d_cells_hbm, sems.at[7]))
    stores[-1].start()

    def tap_step(step, carry):
        lanes = pl.ds(pl.multiple_of(step * 128, 128), 128)
        d = [d_cells[x, :, lanes] for x in range(16)]
        for b in range(7):
            totals = [jnp.zeros((8, 128), F32)] * 7
            for r in range(22):
                cells = shifted[b, r, :, lanes]
                for a in range(max(0, r - 15), min(7, r + 1)):
                    product = cells * d[r - a]
                    totals[a] = totals[a] + product[:8] + product[8:]
            for a in range(7):
                row = a * 7 + b
                small_ref[row : row + 1, lanes] = jnp.sum(totals[a], axis=0, keepdims=True)
        return carry

    lax.fori_loop(0, 4, tap_step, 0)

    half_ref[...] = small_ref[pl.ds(pl.multiple_of(core * 32, 32), 32), :]
    high, low = two_terms(small_ref[pl.ds(pl.multiple_of((1 - core) * 32, 32), 32), :])
    give[2048:2080, :] = high
    give[2080:2112, :] = low
    stores.append(
        pltpu.make_async_copy(give.at[2048:2112], send_hbm.at[2048:2112], sems.at[6])
    )
    stores[-1].start()
    for store in stores:
        store.wait()


def rim_kernel(d_cells, kern_ref, grad_ref, west_ref, east_ref, moved):
    moved[...] = jnp.zeros_like(moved)
    for b in range(7):
        moved[b, :, b : b + 16, :] = d_cells[...]

    def rim_step(step, carry):
        lanes = pl.ds(pl.multiple_of(step * 128, 128), 128)
        for q in range(3):
            rows = slice(q * 8, q * 8 + 8)
            totals = [jnp.zeros((8, 128), F32)] * 22
            for b in range(1 if q == 2 else 0, 7):
                weights = [kern_ref[a * 7 + b : a * 7 + b + 1, lanes] for a in range(7)]
                for x in range(16):
                    cells = moved[b, x, rows, lanes]
                    for a in range(7):
                        totals[x + a] = totals[x + a] + cells * weights[a]
            for i in range(22):
                grad_ref[i, rows, lanes] = totals[i]
        return carry

    lax.fori_loop(0, 4, rim_step, 0)
    filler = jnp.zeros((3, 8, 512), F32)
    west_ref[...] = jnp.concatenate([grad_ref[0:3], filler], axis=1).astype(BF16)
    east_ref[...] = jnp.concatenate([grad_ref[19:22], filler], axis=1).astype(BF16)


MIB = 1024 * 1024
VMEM = pl.BlockSpec(memory_space=pltpu.VMEM)
SMEM = pl.BlockSpec(memory_space=pltpu.SMEM)
HBM = pl.BlockSpec(memory_space=pl.ANY)


def local_call(kernel, name, shapes, in_specs, out_specs, scratch, operands, flops, room):
    return pl.pallas_call(
        kernel,
        out_shape=[jax.ShapeDtypeStruct(s, d) for s, d in shapes],
        in_specs=in_specs,
        out_specs=out_specs,
        scratch_shapes=[pltpu.VMEM(s, d) if d else pltpu.SemaphoreType.DMA(s) for s, d in scratch],
        compiler_params=pltpu.CompilerParams(vmem_limit_bytes=room * MIB),
        cost_estimate=pl.CostEstimate(flops=flops, bytes_accessed=2000000, transcendentals=0),
        name=name,
    )(*operands)


def run_forward(at, ext, kern, gain, w_up, b_up, d_out, d_act, order):
    square, long = (256, 512), (256, 2048)
    return local_call(
        forward_kernel,
        "forward",
        [
            ((16, 16, 512), F32), ((32, 512), F32),
            ((512, 512), F32), ((3, 512, 512), BF16), ((2112, 512), BF16),
        ],
        [SMEM] + [VMEM] * 5 + [HBM] * 3,
        [HBM, VMEM, HBM, HBM, HBM],
        [
            ((22, 32, 512), F32), ((7, 22, 16, 512), F32), (square, BF16), (square, BF16),
            (square, F32), (square, BF16), ((512, 512), F32), (square, F32), ((512, 512), BF16),
            ((512, 2048), BF16), (long, F32), (long, BF16),
            ((512, 512), F32), ((3, 512, 512), BF16), ((2112, 512), BF16), ((64, 512), F32),
            ((16, 16, 512), F32), ((8,), None),
        ],
        [at, ext, kern, gain, b_up, d_out, order, w_up, d_act],
        20000000000,
        56,
    )


def run_rims(d_cells, kern):
    return local_call(
        rim_kernel,
        "rims",
        [((22, 24, 512), F32), ((3, 32, 512), BF16), ((3, 32, 512), BF16)],
        [VMEM] * 2,
        [VMEM] * 3,
        [((7, 16, 24, 512), F32)],
        [d_cells, kern],
        5000000000,
        16,
    )


def run_sum(kernel, shapes, operands, name, scalars=0, scratch=(), room=4):
    return local_call(
        kernel, name, shapes, [SMEM] * scalars + [VMEM] * (len(operands) - scalars),
        [VMEM] * len(shapes), scratch, operands, 800000000, room,
    )


def two_terms(value):
    high = value.astype(BF16)
    return high, (value - high.astype(F32)).astype(BF16)


def rounded(high, low):
    return high.astype(F32) + low.astype(F32)


def whole(first, rest, rows):
    a, b, c = [ref[rows, :].astype(F32) for ref in rest]
    return (first + a) + (b + c)


def whole_terms(first, refs, at):
    a, b, c = [rounded(ref[at : at + 32, :], ref[at + 32 : at + 64, :]) for ref in refs]
    return (first + a) + (b + c)


def first_sum_kernel(mine_ref, keep_ref, given_ref, half_ref, own_ref, terms_ref, *give_refs):
    own_ref[...] = mine_ref[...] + given_ref[0:512, :].astype(F32)
    half = half_ref[...] + rounded(given_ref[2048:2080, :], given_ref[2080:2112, :])
    high, low = two_terms(half)
    terms_ref[...] = rounded(high, low)
    for k in range(3):
        rows = slice(k * 512 + 512, k * 512 + 1024)
        total = keep_ref[k].astype(F32) + given_ref[rows, :].astype(F32)
        give_refs[k][0:512, :] = total.astype(BF16)
        give_refs[k][512:544, :] = high
        give_refs[k][544:576, :] = low


def second_sum_kernel(own_ref, terms_ref, a_ref, b_ref, c_ref, large_ref, next_ref, *give_refs):
    refs = (a_ref, b_ref, c_ref)
    high, low = two_terms(whole_terms(terms_ref[...], refs, 512))
    next_ref[...] = rounded(high, low)
    for k in range(4):
        pieces = [(0, k * 64, 64)] + [(64 + t * 16, 256 + t * 64 + k * 16, 16) for t in range(4)]
        for target, at, count in pieces:
            rows = slice(at, at + count)
            total = whole(own_ref[rows, :], refs, rows)
            if k == 0:
                large_ref[target : target + count, :] = total
            else:
                give_refs[k - 1][target : target + count, :] = total.astype(BF16)
        if k:
            give_refs[k - 1][128:160, :] = high
            give_refs[k - 1][160:192, :] = low


def third_sum_kernel(at_ref, large_ref, terms_ref, a_ref, b_ref, c_ref, *outs):
    refs = (a_ref, b_ref, c_ref)
    own_ref, half_ref, give_refs, blocks = outs[0], outs[1], outs[2:5], outs[5]
    z_at = at_ref[3]
    high, low = two_terms(whole_terms(terms_ref[...], refs, 128))
    half_ref[...] = rounded(high, low)
    down = whole(large_ref[0:64, :], refs, slice(0, 64))
    up = whole(large_ref[64:128, :], refs, slice(64, 128))
    for z in range(8):
        rows = [up[t * 16 + z * 2 : t * 16 + z * 2 + 2] for t in range(4)]
        blocks[z] = jnp.concatenate([down[z * 8 : z * 8 + 8]] + rows, axis=0)
    for k in range(4):
        for part in range(2):
            block = blocks[z_at ^ k ^ (part * 6)]
            rows = slice(part * 16, part * 16 + 16)
            if k == 0:
                own_ref[rows, :] = block
            else:
                give_refs[k - 1][rows, :] = block.astype(BF16)
        if k:
            give_refs[k - 1][32:64, :] = high
            give_refs[k - 1][64:96, :] = low


def fourth_sum_kernel(own_ref, half_ref, a_ref, b_ref, c_ref, keep_ref, sum_ref, give_ref):
    refs = (a_ref, b_ref, c_ref)
    half = whole_terms(half_ref[...], refs, 32)
    keep_ref[...] = whole(own_ref[0:16, :], refs, slice(0, 16))
    give_ref[0:16, :] = whole(own_ref[16:32, :], refs, slice(16, 32))
    give_ref[16:48, :] = half
    sum_ref[...] = half


def last_sum_kernel(keep_ref, half_ref, got_ref, down_ref, up_ref, sum_ref):
    sum_ref[...] = half_ref[...] + got_ref[16:48, :]
    down_ref[...] = keep_ref[0:8, :] + got_ref[0:8, :]
    up = keep_ref[8:16, :] + got_ref[8:16, :]
    for t in range(4):
        up_ref[:, t * 512 : t * 512 + 512] = up[t * 2 : t * 2 + 2]


def split_kernel(at_ref, half_ref, other_ref, kernel_ref, gain_ref, bias_ref):
    first = at_ref[0] == 0
    half, other = half_ref[...], other_ref[...]
    low, high = jnp.where(first, half, other), jnp.where(first, other, half)
    kernel_ref[0:32, :] = low
    kernel_ref[32:49, :] = high[0:17]
    gain_ref[...] = high[17:18]
    for t in range(4):
        bias_ref[:, t * 512 : t * 512 + 512] = high[18 + t : 19 + t]


def per_device(
    field, cotangent, land_sea, fold_partner, depth_kernel, norm_gain, w_up, b_up, w_down
):
    width_lon, width_lat, channels = field.shape
    lon_at = lax.axis_index("lon")
    lat_at = lax.axis_index("lat")
    core = lon_at & 1
    z_at = (lon_at >> 1) & 7
    y_at = ((lat_at >> 2) << 1) + (lon_at >> 4)
    x_at = lat_at & 3
    is_north = lat_at == lax.axis_size("lat") - 1
    from_end = 511 - fold_partner[0]
    turn = 31 - (from_end >> 4)
    shift = 16 - (from_end & 15)
    even = (turn & 1) == 0

    top_rows = field[:, width_lat - 3 :, :]
    mine, south, north = mirror_tiles(
        top_rows, turn >> 1, (top_rows, field[:, 0:3, :]), lambda a, b: (to_north(a), to_south(b))
    )
    low = jnp.where(even, top_to_previous(mine), mine)
    high = jnp.where(even, mine, top_to_next(mine))
    fold = lax.dynamic_slice_in_dim(jnp.concatenate([low, high], axis=0), shift, 16, axis=0)
    north = jnp.where(is_north, fold[::-1, ::-1, :], north)
    column = jnp.concatenate([south, field, north], axis=1)
    extended = jnp.concatenate(
        [to_next(column[width_lon - 3 :]), column, to_previous(column[:3])], axis=0
    )
    extended = jnp.pad(extended, ((0, 0), (0, 10), (0, 0)))
    tokens = width_lon * width_lat
    d_out = cotangent.reshape(tokens, channels) * land_sea.reshape(tokens, 1).astype(jnp.bfloat16)
    d_act = lax.dot_general(
        d_out, w_down, (((1,), (1,)), ((), ())), preferred_element_type=jnp.float32
    )
    row = jnp.arange(512, dtype=jnp.int32)
    block = row >> 1
    y_of = (((block >> 2) & 1) << 1) + (block >> 7)
    goes_to = (
        (((block >> 3) & 1) ^ core) * 256
        + ((block & 3) ^ x_at) * 64
        + (y_of ^ y_at) * 16
        + ((block >> 4) & 7) * 2
        + (row & 1)
    )
    order = (goes_to[:, None] == row[None, :]).astype(jnp.bfloat16)
    at = jnp.stack([core, x_at, y_at, z_at]).astype(jnp.int32)
    gain = norm_gain.reshape(1, channels)
    d_cells, half, mine, keep, give = run_forward(
        at, extended, depth_kernel, gain, w_up, b_up.reshape(1, 2048), d_out, d_act, order
    )

    given = send(give, CORE_MASK)
    grad_ext, west_rim, east_rim = run_rims(d_cells, depth_kernel)
    given, west_rim, east_rim = lax.optimization_barrier((given, west_rim, east_rim))
    own, terms, *give = run_sum(
        first_sum_kernel,
        [((512, 512), F32), ((32, 512), F32)] + [((576, 512), BF16)] * 3,
        [mine, keep, given, half],
        "first_sum",
        room=16,
    )
    taken = [send(piece, mask) for piece, mask in zip(give, X_MASKS)]

    rim = jnp.bfloat16
    from_west, from_east = to_next(east_rim), to_previous(west_rim)
    from_west, from_east = from_west[:, :22].astype(F32), from_east[:, :22].astype(F32)
    by_cols = (
        grad_ext[3:19, :22]
        + jnp.pad(from_west, ((0, 13), (0, 0), (0, 0)))
        + jnp.pad(from_east, ((13, 0), (0, 0), (0, 0)))
    )
    top_rim = by_cols[:, 19:22].astype(rim)
    from_south = to_north(top_rim)
    from_north = to_south(by_cols[:, 0:3].astype(rim))
    strip = jnp.where(is_north, top_rim, jnp.zeros_like(top_rim))[::-1, ::-1, :]
    spread = lax.dynamic_update_slice_in_dim(
        jnp.zeros((32, 3, channels), rim), strip, shift, axis=0
    )
    none = jnp.zeros_like(spread[:16])
    mine = jnp.where(even, spread[16:], spread[:16])
    mine = mine + top_to_next(jnp.where(even, spread[:16], none))
    mine = mine + top_to_previous(jnp.where(even, none, spread[16:]))
    mine, from_south, from_north, taken = lax.optimization_barrier(
        (mine, from_south, from_north, taken)
    )

    large, terms, *give = run_sum(
        second_sum_kernel,
        [((128, 512), F32), ((32, 512), F32)] + [((192, 512), BF16)] * 3,
        [own, terms, *taken],
        "second_sum",
        room=8,
    )
    taken = [send(piece, mask) for piece, mask in zip(give, Y_MASKS)]

    own, half, *give = run_sum(
        third_sum_kernel,
        [((32, 512), F32), ((32, 512), F32)] + [((96, 512), BF16)] * 3,
        [at, large, terms, *taken],
        "third_sum",
        scalars=1,
        scratch=[((8, 16, 512), F32)],
    )
    taken = [send(piece, mask) for piece, mask in zip(give, Z_MASKS[:3])]
    keep, half, give = run_sum(
        fourth_sum_kernel,
        [((16, 512), F32), ((32, 512), F32), ((48, 512), F32)],
        [own, half, *taken],
        "fourth_sum",
    )
    from_fold, got = mirror_tiles(mine, turn >> 1, (give,), lambda v: (send(v, Z_MASKS[3]),))
    from_fold = from_fold.astype(F32)
    grad_down, grad_up, half = run_sum(
        last_sum_kernel,
        [((8, 512), F32), ((2, 2048), F32), ((32, 512), F32)],
        [keep, half, got],
        "last_sum",
    )
    other = send(half, CORE_MASK)
    grad_kernel, grad_gain, grad_bias = run_sum(
        split_kernel,
        [((49, 512), F32), ((1, 512), F32), ((1, 2048), F32)],
        [at, half, other],
        "split",
        scalars=1,
    )
    grad_gain = grad_gain.reshape(512)
    grad_bias = grad_bias.reshape(2048)
    owned = by_cols[:, 3:19] + jnp.pad(from_south.astype(F32), ((0, 0), (0, 13), (0, 0)))
    owned = owned + jnp.pad(from_north.astype(F32) + from_fold, ((0, 0), (13, 0), (0, 0)))
    grad_field = (cotangent.astype(F32) + owned).astype(jnp.bfloat16)
    return (grad_field, grad_up, grad_down, grad_kernel, grad_gain, grad_bias)


def solution(mesh):
    placed = (
        P("lon", "lat", None),
        P("lon", "lat", None),
        P("lon", "lat"),
        P(),
        P(),
        P(),
        P(),
        P(),
        P(),
    )
    return jax.shard_map(
        per_device,
        mesh=mesh,
        in_specs=placed,
        out_specs=(
            P("lon", "lat", None),
            P(("lon", "lat"), None),
            P(("lon", "lat"), None),
            P(),
            P(),
            P(),
        ),
        check_vma=False,
    )
```

profile of v0, /device:TPU:65, one launch (start us, length us, event | category | flops | bytes accessed | tf_op | source)
XLA Modules:
  0.0 142.3 jit_solution(8042271977631409541)
XLA Ops:
  0.6 1.3 slice.43
  2.0 1.0 fusion.16
  3.7 10.1 %conditional.4 = (bf16[16,3,512]{2,1,0:T(4,128)(2,1)}, bf16[16,3,512]{2,1,0:T(4,128)(2,1)}, bf16[16,3,512]{2,1,0:T(4,128)(2,1)}) conditional(s32[]{:T(128)} %bitcast.4, (bf16[16,3,512]{2,1,0:T(4,128)(2,1)S(1)}, bf16[16,3,512]{2,1,0:T(4,128)(2,1)S(1)}) %tuple.204, (bf16[16,3,512]{2,1,0:T(4,128)(2,1)S(1)}, ...), branch_computations={%region_0.0_spmd, %region_1.0_spmd, %region_2.0_spmd, %region_3.0_... | conditional | bytes 589968 | solution.py:50
  3.7 1.3 collective-permute-start.3
  5.0 3.7 %collective-permute-start.4 = (bf16[16,3,512]{2,1,0:T(4,128)(2,1)S(1)}, bf16[16,3,512]{2,1,0:T(4,128)(2,1)}, u32[]{:S(2)}, u32[]{:S(2)}) collective-permute-start(bf16[16,3,512]{2,1,0:T(4,128)(2,1)S(1)} %get-tuple-element.138), channel_id=1, source_target_pairs={{0,1},{1,2},{2,3},{3,4},{4,5},{5,6},{6,7},{8,9},{9,10},{10,11},{11... | collective-permute-start | bytes 147464 | tf_op jit(solution)/shard_map/cond/branch_1_fun/ppermute | solution.py:28
  8.7 1.3 collective-permute-start.5
  10.0 3.8 %collective-permute-done.5 = bf16[16,3,512]{2,1,0:T(4,128)(2,1)} collective-permute-done((bf16[16,3,512]{2,1,0:T(4,128)(2,1)S(1)}, bf16[16,3,512]{2,1,0:T(4,128)(2,1)}, u32[]{:S(2)}, u32[]{:S(2)}) %collective-permute-start.5) | collective-permute-done | bytes 49184 | tf_op jit(solution)/shard_map/cond/branch_1_fun/ppermute | solution.py:32
  13.8 0.7 collective-permute-start.80
  14.5 0.7 collective-permute-start.81
  15.1 0.7 convert_element_type.76
  15.9 0.1 convert_element_type.77
  15.9 1.1 bitcast_multiply_fusion.d_out_ref
  17.0 2.1 %fusion.17.d_act_hbm = f32[256,2048]{1,0:T(8,128)} fusion(bf16[256,512]{1,0:T(8,128)(2,1)S(1)} %bitcast_multiply_fusion.d_out_ref, bf16[2048,512]{1,0:T(8,128)(2,1)S(1)} %copy-done), kind=kOutput, calls=%fused_computation.38 | convolution fusion | flops 536870912 | bytes 4456448 | tf_op jit(solution)/shard_map/dot_general | solution.py:444
  19.1 1.0 fusion.5.order_hbm
  20.1 0.9 broadcast_select_fusion.2
  21.0 0.1 fusion.13
  21.1 0.2 rev.6
  21.4 0.9 broadcast_select_fusion.5
  22.3 0.8 pad_maximum_fusion.2
  23.1 3.7 %collective-permute-start.82 = (bf16[3,22,512]{2,1,0:T(8,128)(2,1)S(1)}, bf16[3,22,512]{2,1,0:T(8,128)(2,1)S(1)}, u32[]{:S(2)}, u32[]{:S(2)}) collective-permute-start(bf16[3,22,512]{2,1,0:T(8,128)(2,1)S(1)} %get-tuple-element.307), channel_id=1, source_target_pairs={{0,8},{8,16},{16,24},{24,32},{32,40},{40,48},{48,56},{56,64},{64,7... | collective-permute-start | bytes 202760 | tf_op jit(solution)/shard_map/ppermute | solution.py:20
  26.8 0.6 pad_add_fusion.at_ref
  27.4 0.8 collective-permute-done.82
  28.2 2.4 %collective-permute-done.83 = bf16[3,22,512]{2,1,0:T(8,128)(2,1)S(1)} collective-permute-done((bf16[3,22,512]{2,1,0:T(8,128)(2,1)S(1)}, bf16[3,22,512]{2,1,0:T(8,128)(2,1)S(1)}, u32[]{:S(2)}, u32[]{:S(2)}) %collective-permute-start.83) | collective-permute-done | bytes 67616 | tf_op jit(solution)/shard_map/ppermute | solution.py:24
  30.5 2.0 %fusion.7.ext_ref = bf16[22,32,512]{2,1,0:T(8,128)(2,1)} fusion(bf16[3,22,512]{2,1,0:T(8,128)(2,1)S(1)} %collective-permute-done.83, bf16[3,22,512]{2,1,0:T(8,128)(2,1)S(1)} %collective-permute-done.82, bf16[16,3,512]{2,1,0:T(4,128)(2,1)S(1)} %broadcast_select_fusion.5, bf16[16,16,512]{2,1,0:T(8,128)(2,1)S(1)} %copy-done.8, ...), kind=kLoop, calls=%fused_computation.10 | loop fusion | flops 5767168 | bytes 1216512 | tf_op jit(solution)/shard_map/concatenate | solution.py:438
  32.6 17.7 %forward.1 = (f32[16,16,512]{2,1,0:T(8,128)}, f32[32,512]{1,0:T(8,128)}, f32[512,512]{1,0:T(8,128)}, bf16[3,512,512]{2,1,0:T(8,128)(2,1)}, bf16[2112,512]{1,0:T(8,128)(2,1)}) custom-call(s32[4]{0:T(128)} %pad_add_fusion.at_ref, bf16[22,32,512]{2,1,0:T(8,128)(2,1)} %fusion.7.ext_ref, f32[49,512]{1,0:T(8,128)} %kern_ref.3, f32[1,512]{1,0:T(1,128)} %bitcast.17, ...), custom_call_target="tpu_custom_call" | custom-call | flops 20000000000 | bytes 2000000 | tf_op jit(solution)/shard_map/forward/pallas_call | solution.py:254
  50.3 0.3 collective-permute-start.84
  50.6 1.0 copy-done.6
  51.6 3.8 %rims.1 = (f32[22,24,512]{2,1,0:T(8,128)S(1)}, bf16[3,32,512]{2,1,0:T(8,128)(2,1)S(1)}, bf16[3,32,512]{2,1,0:T(8,128)(2,1)S(1)}) custom-call(f32[16,16,512]{2,1,0:T(8,128)S(1)} %copy-done.6, f32[49,512]{1,0:T(8,128)S(1)} %copy-done.5), custom_call_target="tpu_custom_call" | custom-call | flops 5000000000 | bytes 2000000 | tf_op jit(solution)/shard_map/rims/pallas_call | solution.py:254
  55.5 4.5 %collective-permute-start.85 = (bf16[3,32,512]{2,1,0:T(8,128)(2,1)S(1)}, bf16[3,32,512]{2,1,0:T(8,128)(2,1)S(1)}, u32[]{:S(2)}, u32[]{:S(2)}) collective-permute-start(bf16[3,32,512]{2,1,0:T(8,128)(2,1)S(1)} %get-tuple-element.260), channel_id=1, source_target_pairs={{0,8},{8,16},{16,24},{24,32},{32,40},{40,48},{48,56},{56,64},{64,7... | collective-permute-start | bytes 294920 | tf_op jit(solution)/shard_map/ppermute | solution.py:20
  60.0 1.3 first_sum.1
  61.3 0.6 collective-permute-start.91
  62.0 7.7 %collective-permute-start.92 = (bf16[576,512]{1,0:T(8,128)(2,1)}, bf16[576,512]{1,0:T(8,128)(2,1)}, u32[]{:S(2)}, u32[]{:S(2)}) collective-permute-start(bf16[576,512]{1,0:T(8,128)(2,1)} %get-tuple-element.267), channel_id=1, source_target_pairs={{0,2},{1,3},{2,0},{3,1},{4,6},{5,7},{6,4},{7,5},{8,10},{9,11},{10,... | collective-permute-start | bytes 1769480 | tf_op jit(solution)/shard_map/ppermute | solution.py:16
  69.7 1.1 fusion.14
  70.8 0.2 rev.7
  71.2 0.7 collective-permute-start.87
  71.9 0.7 collective-permute-start.88
  72.6 1.6 %collective-permute-start.89 = (bf16[16,3,512]{2,1,0:T(4,128)(2,1)S(1)}, bf16[16,3,512]{2,1,0:T(4,128)(2,1)S(1)}, u32[]{:S(2)}, u32[]{:S(2)}) collective-permute-start(bf16[16,3,512]{2,1,0:T(4,128)(2,1)S(1)} %get-tuple-element.306), channel_id=1, source_target_pairs={{0,1},{1,2},{2,3},{3,4},{4,5},{5,6},{6,7},{8,9},{9,10},{10,11},{11... | collective-permute-start | bytes 147464 | tf_op jit(solution)/shard_map/ppermute | solution.py:28
  74.2 1.3 collective-permute-start.90
  75.5 12.1 %collective-permute-done.89 = bf16[16,3,512]{2,1,0:T(4,128)(2,1)S(1)} collective-permute-done((bf16[16,3,512]{2,1,0:T(4,128)(2,1)S(1)}, bf16[16,3,512]{2,1,0:T(4,128)(2,1)S(1)}, u32[]{:S(2)}, u32[]{:S(2)}) %collective-permute-start.89) | collective-permute-done | bytes 49184 | tf_op jit(solution)/shard_map/ppermute | solution.py:28
  87.7 1.7 %collective-permute-done.90 = bf16[16,3,512]{2,1,0:T(4,128)(2,1)S(1)} collective-permute-done((bf16[16,3,512]{2,1,0:T(4,128)(2,1)S(1)}, bf16[16,3,512]{2,1,0:T(4,128)(2,1)S(1)}, u32[]{:S(2)}, u32[]{:S(2)}) %collective-permute-start.90) | collective-permute-done | bytes 49184 | tf_op jit(solution)/shard_map/ppermute | solution.py:32
  89.3 5.9 %collective-permute-done.92.b_ref = bf16[576,512]{1,0:T(8,128)(2,1)} collective-permute-done((bf16[576,512]{1,0:T(8,128)(2,1)}, bf16[576,512]{1,0:T(8,128)(2,1)}, u32[]{:S(2)}, u32[]{:S(2)}) %collective-permute-start.92) | collective-permute-done | bytes 589856 | tf_op jit(solution)/shard_map/ppermute | solution.py:16
  95.2 3.1 %collective-permute-done.93.c_ref = bf16[576,512]{1,0:T(8,128)(2,1)} collective-permute-done((bf16[576,512]{1,0:T(8,128)(2,1)}, bf16[576,512]{1,0:T(8,128)(2,1)}, u32[]{:S(2)}, u32[]{:S(2)}) %collective-permute-start.93) | collective-permute-done | bytes 589856 | tf_op jit(solution)/shard_map/ppermute | solution.py:16
  98.4 1.7 %second_sum.1 = (f32[128,512]{1,0:T(8,128)S(1)}, f32[32,512]{1,0:T(8,128)S(1)}, bf16[192,512]{1,0:T(8,128)(2,1)S(1)}, bf16[192,512]{1,0:T(8,128)(2,1)S(1)}, bf16[192,512]{1,0:T(8,128)(2,1)S(1)}) custom-call(f32[512,512]{1,0:T(8,128)S(1)} %get-tuple-element.271.own_ref, f32[32,512]{1,0:T(8,128)S(1)} %get-tuple-element.272.terms_ref, ...), custom_call_target="tpu_custom_call" | custom-call | flops 800000000 | bytes 2000000 | tf_op jit(solution)/shard_map/second_sum/pallas_call | solution.py:254
  100.1 0.5 collective-permute-start.94
  100.6 3.9 %collective-permute-start.95 = (bf16[192,512]{1,0:T(8,128)(2,1)S(1)}, bf16[192,512]{1,0:T(8,128)(2,1)S(1)}, u32[]{:S(2)}, u32[]{:S(2)}) collective-permute-start(bf16[192,512]{1,0:T(8,128)(2,1)S(1)} %get-tuple-element.279), channel_id=1, source_target_pairs={{0,4},{1,5},{2,6},{3,7},{4,0},{5,1},{6,2},{7,3},{8,12},{9,13},{10,... | collective-permute-start | bytes 589832 | tf_op jit(solution)/shard_map/ppermute | solution.py:16
  104.5 2.0 %collective-permute-done.94.a_ref = bf16[192,512]{1,0:T(8,128)(2,1)S(1)} collective-permute-done((bf16[192,512]{1,0:T(8,128)(2,1)S(1)}, bf16[192,512]{1,0:T(8,128)(2,1)S(1)}, u32[]{:S(2)}, u32[]{:S(2)}) %collective-permute-start.94) | collective-permute-done | bytes 196640 | tf_op jit(solution)/shard_map/ppermute | solution.py:16
  106.5 7.6 %collective-permute-done.95.b_ref = bf16[192,512]{1,0:T(8,128)(2,1)S(1)} collective-permute-done((bf16[192,512]{1,0:T(8,128)(2,1)S(1)}, bf16[192,512]{1,0:T(8,128)(2,1)S(1)}, u32[]{:S(2)}, u32[]{:S(2)}) %collective-permute-start.95) | collective-permute-done | bytes 196640 | tf_op jit(solution)/shard_map/ppermute | solution.py:16
  114.1 2.3 %collective-permute-done.96.c_ref = bf16[192,512]{1,0:T(8,128)(2,1)S(1)} collective-permute-done((bf16[192,512]{1,0:T(8,128)(2,1)S(1)}, bf16[192,512]{1,0:T(8,128)(2,1)S(1)}, u32[]{:S(2)}, u32[]{:S(2)}) %collective-permute-start.96) | collective-permute-done | bytes 196640 | tf_op jit(solution)/shard_map/ppermute | solution.py:16
  116.4 0.7 third_sum.1
  117.1 0.1 collective-permute-start.97
  117.2 0.1 collective-permute-start.98
  117.3 2.5 %collective-permute-start.99 = (bf16[96,512]{1,0:T(8,128)(2,1)S(1)}, bf16[96,512]{1,0:T(8,128)(2,1)S(1)}, u32[]{:S(2)}, u32[]{:S(2)}) collective-permute-start(bf16[96,512]{1,0:T(8,128)(2,1)S(1)} %get-tuple-element.285), channel_id=1, source_target_pairs={{0,48},{1,49},{2,50},{3,51},{4,52},{5,53},{6,54},{7,55},{8,56},{9,... | collective-permute-start | bytes 294920 | tf_op jit(solution)/shard_map/ppermute | solution.py:16
  119.9 0.8 collective-permute-done.97.a_ref
  120.7 1.1 collective-permute-done.98.b_ref
  121.8 7.5 %collective-permute-done.99.c_ref = bf16[96,512]{1,0:T(8,128)(2,1)S(1)} collective-permute-done((bf16[96,512]{1,0:T(8,128)(2,1)S(1)}, bf16[96,512]{1,0:T(8,128)(2,1)S(1)}, u32[]{:S(2)}, u32[]{:S(2)}) %collective-permute-start.99) | collective-permute-done | bytes 98336 | tf_op jit(solution)/shard_map/ppermute | solution.py:16
  129.3 8.0 %conditional.6 = (f32[48,512]{1,0:T(8,128)}, bf16[16,3,512]{2,1,0:T(4,128)(2,1)}) conditional(s32[]{:T(128)} %bitcast.4, (f32[48,512]{1,0:T(8,128)S(1)}, bf16[16,3,512]{2,1,0:T(4,128)(2,1)S(1)}) %tuple.207, (f32[48,512]{1,0:T(8,128)S(1)}, bf16[16,3,512]{2,1,0:T(4,128)(2,1)S(1)}) %tuple.207, (f32[48,512]{1,0:T(8,128)S(1)}, ...), branch_computations={%region_16.17_spmd, %region_17.18_spmd, %region_18.19_spmd, %regio... | conditional | bytes 589920
  129.3 0.1 collective-permute-start.50
  129.4 1.3 collective-permute-start.51
  130.7 6.5 %collective-permute-done.50 = f32[48,512]{1,0:T(8,128)} collective-permute-done((f32[48,512]{1,0:T(8,128)S(1)}, f32[48,512]{1,0:T(8,128)}, u32[]{:S(2)}, u32[]{:S(2)}) %collective-permute-start.50) | collective-permute-done | bytes 98336 | tf_op jit(solution)/shard_map/cond/branch_1_fun/ppermute | solution.py:16
  137.3 1.6 %last_sum.1 = (f32[8,512]{1,0:T(8,128)}, f32[2,2048]{1,0:T(2,128)}, f32[32,512]{1,0:T(8,128)S(1)}) custom-call(f32[16,512]{1,0:T(8,128)S(1)} %get-tuple-element.289.keep_ref, f32[32,512]{1,0:T(8,128)S(1)} %get-tuple-element.290.half_ref, f32[48,512]{1,0:T(8,128)} %get-tuple-element.291.got_ref), custom_call_target="tpu_custom_call" | custom-call | flops 800000000 | bytes 2000000 | tf_op jit(solution)/shard_map/last_sum/pallas_call | solution.py:254
  138.8 0.5 collective-permute-start.100
  139.3 0.9 convert_add_fusion.1
  140.2 0.9 fusion.12
  141.1 1.2 split.1
  (46 shorter events, 0.4 us)
Async XLA Ops:
  0.6 16.4 %copy-start = (bf16[2048,512]{1,0:T(8,128)(2,1)S(1)}, bf16[2048,512]{1,0:T(8,128)(2,1)}, u32[]{:S(2)}) copy-start(bf16[2048,512]{1,0:T(8,128)(2,1)} %param.49) | copy-start | bytes 6291460
  3.7 6.3 %collective-permute-start.3 = (bf16[16,3,512]{2,1,0:T(4,128)(2,1)S(1)}, bf16[16,3,512]{2,1,0:T(4,128)(2,1)}, u32[]{:S(2)}, u32[]{:S(2)}) collective-permute-start(bf16[16,3,512]{2,1,0:T(4,128)(2,1)S(1)} %get-tuple-element.138), channel_id=1, source_target_pairs={{7,23},{15,15},{23,7},{31,255},{39,247},{47,239},{55,231},{63,223}... | collective-permute-start | bytes 147464 | tf_op jit(solution)/shard_map/cond/branch_1_fun/ppermute | solution.py:48
  5.0 5.0 %collective-permute-start.4 = (bf16[16,3,512]{2,1,0:T(4,128)(2,1)S(1)}, bf16[16,3,512]{2,1,0:T(4,128)(2,1)}, u32[]{:S(2)}, u32[]{:S(2)}) collective-permute-start(bf16[16,3,512]{2,1,0:T(4,128)(2,1)S(1)} %get-tuple-element.138), channel_id=1, source_target_pairs={{0,1},{1,2},{2,3},{3,4},{4,5},{5,6},{6,7},{8,9},{9,10},{10,11},{11... | collective-permute-start | bytes 147464 | tf_op jit(solution)/shard_map/cond/branch_1_fun/ppermute | solution.py:28
  8.7 5.1 %collective-permute-start.5 = (bf16[16,3,512]{2,1,0:T(4,128)(2,1)S(1)}, bf16[16,3,512]{2,1,0:T(4,128)(2,1)}, u32[]{:S(2)}, u32[]{:S(2)}) collective-permute-start(bf16[16,3,512]{2,1,0:T(4,128)(2,1)S(1)} %get-tuple-element.139), channel_id=1, source_target_pairs={{1,0},{2,1},{3,2},{4,3},{5,4},{6,5},{7,6},{9,8},{10,9},{11,10},{12... | collective-permute-start | bytes 147464 | tf_op jit(solution)/shard_map/cond/branch_1_fun/ppermute | solution.py:32
  13.8 6.3 %collective-permute-start.80 = (bf16[16,3,512]{2,1,0:T(4,128)(2,1)}, bf16[16,3,512]{2,1,0:T(4,128)(2,1)S(1)}, u32[]{:S(2)}, u32[]{:S(2)}) collective-permute-start(bf16[16,3,512]{2,1,0:T(4,128)(2,1)} %get-tuple-element.253), channel_id=1, source_target_pairs={{15,7},{23,15},{31,23},{39,31},{47,39},{55,47},{63,55},{71,63},{79... | collective-permute-start | bytes 147464 | tf_op jit(solution)/shard_map/ppermute | solution.py:42
  14.5 5.6 %collective-permute-start.81 = (bf16[16,3,512]{2,1,0:T(4,128)(2,1)}, bf16[16,3,512]{2,1,0:T(4,128)(2,1)S(1)}, u32[]{:S(2)}, u32[]{:S(2)}) collective-permute-start(bf16[16,3,512]{2,1,0:T(4,128)(2,1)} %get-tuple-element.253), channel_id=1, source_target_pairs={{7,15},{15,23},{23,31},{31,39},{39,47},{47,55},{55,63},{63,71},{71... | collective-permute-start | bytes 147464 | tf_op jit(solution)/shard_map/ppermute | solution.py:37
  17.0 2.1 %copy-start.10 = (bf16[256,512]{1,0:T(8,128)(2,1)}, bf16[256,512]{1,0:T(8,128)(2,1)S(1)}, u32[]{:S(2)}) copy-start(bf16[256,512]{1,0:T(8,128)(2,1)S(1)} %bitcast_multiply_fusion.d_out_ref) | copy-start | bytes 786436
  19.1 3.2 %copy-start.8 = (bf16[16,16,512]{2,1,0:T(8,128)(2,1)S(1)}, bf16[16,16,512]{2,1,0:T(8,128)(2,1)}, u32[]{:S(2)}) copy-start(bf16[16,16,512]{2,1,0:T(8,128)(2,1)} %param.41) | copy-start | bytes 786436
  23.1 5.1 %collective-permute-start.82 = (bf16[3,22,512]{2,1,0:T(8,128)(2,1)S(1)}, bf16[3,22,512]{2,1,0:T(8,128)(2,1)S(1)}, u32[]{:S(2)}, u32[]{:S(2)}) collective-permute-start(bf16[3,22,512]{2,1,0:T(8,128)(2,1)S(1)} %get-tuple-element.307), channel_id=1, source_target_pairs={{0,8},{8,16},{16,24},{24,32},{32,40},{40,48},{48,56},{56,64},{64,7... | collective-permute-start | bytes 202760 | tf_op jit(solution)/shard_map/ppermute | solution.py:20
  26.8 3.8 %collective-permute-start.83 = (bf16[3,22,512]{2,1,0:T(8,128)(2,1)S(1)}, bf16[3,22,512]{2,1,0:T(8,128)(2,1)S(1)}, u32[]{:S(2)}, u32[]{:S(2)}) collective-permute-start(bf16[3,22,512]{2,1,0:T(8,128)(2,1)S(1)} %get-tuple-element.308), channel_id=1, source_target_pairs={{8,0},{16,8},{24,16},{32,24},{40,32},{48,40},{56,48},{64,56},{72,6... | collective-permute-start | bytes 202760 | tf_op jit(solution)/shard_map/ppermute | solution.py:24
  32.6 18.0 %copy-start.5 = (f32[49,512]{1,0:T(8,128)S(1)}, f32[49,512]{1,0:T(8,128)}, u32[]{:S(2)}) copy-start(f32[49,512]{1,0:T(8,128)} %kern_ref.3) | copy-start | bytes 301060
  50.3 5.2 %collective-permute-start.84 = (bf16[2112,512]{1,0:T(8,128)(2,1)}, bf16[2112,512]{1,0:T(8,128)(2,1)S(1)}, u32[]{:S(2)}, u32[]{:S(2)}) collective-permute-start(bf16[2112,512]{1,0:T(8,128)(2,1)} %get-tuple-element.257), channel_id=1, source_target_pairs={{0,8},{1,9},{2,10},{3,11},{4,12},{5,13},{6,14},{7,15},{8,0},{9,1},... | collective-permute-start | bytes 6488072 | tf_op jit(solution)/shard_map/ppermute | solution.py:16
  50.6 1.0 copy-start.6
  51.6 8.3 %copy-start.1 = (bf16[3,512,512]{2,1,0:T(8,128)(2,1)S(1)}, bf16[3,512,512]{2,1,0:T(8,128)(2,1)}, u32[]{:S(2)}) copy-start(bf16[3,512,512]{2,1,0:T(8,128)(2,1)} %get-tuple-element.263.keep_ref) | copy-start | bytes 4718596
  51.6 8.3 %copy-start.2 = (f32[512,512]{1,0:T(8,128)S(1)}, f32[512,512]{1,0:T(8,128)}, u32[]{:S(2)}) copy-start(f32[512,512]{1,0:T(8,128)} %get-tuple-element.262.mine_ref) | copy-start | bytes 3145732
  51.6 8.3 %copy-start.3 = (f32[32,512]{1,0:T(8,128)S(1)}, f32[32,512]{1,0:T(8,128)}, u32[]{:S(2)}) copy-start(f32[32,512]{1,0:T(8,128)} %get-tuple-element.265.half_ref) | copy-start | bytes 196612
  55.5 14.2 %collective-permute-start.85 = (bf16[3,32,512]{2,1,0:T(8,128)(2,1)S(1)}, bf16[3,32,512]{2,1,0:T(8,128)(2,1)S(1)}, u32[]{:S(2)}, u32[]{:S(2)}) collective-permute-start(bf16[3,32,512]{2,1,0:T(8,128)(2,1)S(1)} %get-tuple-element.260), channel_id=1, source_target_pairs={{0,8},{8,16},{16,24},{24,32},{32,40},{40,48},{48,56},{56,64},{64,7... | collective-permute-start | bytes 294920 | tf_op jit(solution)/shard_map/ppermute | solution.py:20
  60.0 9.7 %collective-permute-start.86 = (bf16[3,32,512]{2,1,0:T(8,128)(2,1)S(1)}, bf16[3,32,512]{2,1,0:T(8,128)(2,1)S(1)}, u32[]{:S(2)}, u32[]{:S(2)}) collective-permute-start(bf16[3,32,512]{2,1,0:T(8,128)(2,1)S(1)} %get-tuple-element.261), channel_id=1, source_target_pairs={{8,0},{16,8},{24,16},{32,24},{40,32},{48,40},{56,48},{64,56},{72,6... | collective-permute-start | bytes 294920 | tf_op jit(solution)/shard_map/ppermute | solution.py:24
  61.3 28.0 %collective-permute-start.91 = (bf16[576,512]{1,0:T(8,128)(2,1)}, bf16[576,512]{1,0:T(8,128)(2,1)}, u32[]{:S(2)}, u32[]{:S(2)}) collective-permute-start(bf16[576,512]{1,0:T(8,128)(2,1)} %get-tuple-element.266), channel_id=1, source_target_pairs={{0,1},{1,0},{2,3},{3,2},{4,5},{5,4},{6,7},{7,6},{8,9},{9,8},{10,11... | collective-permute-start | bytes 1769480 | tf_op jit(solution)/shard_map/ppermute | solution.py:16
  62.0 33.3 %collective-permute-start.92 = (bf16[576,512]{1,0:T(8,128)(2,1)}, bf16[576,512]{1,0:T(8,128)(2,1)}, u32[]{:S(2)}, u32[]{:S(2)}) collective-permute-start(bf16[576,512]{1,0:T(8,128)(2,1)} %get-tuple-element.267), channel_id=1, source_target_pairs={{0,2},{1,3},{2,0},{3,1},{4,6},{5,7},{6,4},{7,5},{8,10},{9,11},{10,... | collective-permute-start | bytes 1769480 | tf_op jit(solution)/shard_map/ppermute | solution.py:16
  69.6 28.7 %collective-permute-start.93 = (bf16[576,512]{1,0:T(8,128)(2,1)}, bf16[576,512]{1,0:T(8,128)(2,1)}, u32[]{:S(2)}, u32[]{:S(2)}) collective-permute-start(bf16[576,512]{1,0:T(8,128)(2,1)} %get-tuple-element.268), channel_id=1, source_target_pairs={{0,3},{1,2},{2,1},{3,0},{4,7},{5,6},{6,5},{7,4},{8,11},{9,10},{10,... | collective-permute-start | bytes 1769480 | tf_op jit(solution)/shard_map/ppermute | solution.py:16
  71.2 1.3 collective-permute-start.87
  71.9 2.3 %collective-permute-start.88 = (bf16[16,3,512]{2,1,0:T(4,128)(2,1)S(1)}, bf16[16,3,512]{2,1,0:T(4,128)(2,1)S(1)}, u32[]{:S(2)}, u32[]{:S(2)}) collective-permute-start(bf16[16,3,512]{2,1,0:T(4,128)(2,1)S(1)} %get-tuple-element.312), channel_id=1, source_target_pairs={{15,7},{23,15},{31,23},{39,31},{47,39},{55,47},{63,55},{71,63},{79... | collective-permute-start | bytes 147464 | tf_op jit(solution)/shard_map/ppermute | solution.py:42
  72.6 15.1 %collective-permute-start.89 = (bf16[16,3,512]{2,1,0:T(4,128)(2,1)S(1)}, bf16[16,3,512]{2,1,0:T(4,128)(2,1)S(1)}, u32[]{:S(2)}, u32[]{:S(2)}) collective-permute-start(bf16[16,3,512]{2,1,0:T(4,128)(2,1)S(1)} %get-tuple-element.306), channel_id=1, source_target_pairs={{0,1},{1,2},{2,3},{3,4},{4,5},{5,6},{6,7},{8,9},{9,10},{10,11},{11... | collective-permute-start | bytes 147464 | tf_op jit(solution)/shard_map/ppermute | solution.py:28
  74.2 15.2 %collective-permute-start.90 = (bf16[16,3,512]{2,1,0:T(4,128)(2,1)S(1)}, bf16[16,3,512]{2,1,0:T(4,128)(2,1)S(1)}, u32[]{:S(2)}, u32[]{:S(2)}) collective-permute-start(bf16[16,3,512]{2,1,0:T(4,128)(2,1)S(1)} %get-tuple-element.304), channel_id=1, source_target_pairs={{1,0},{2,1},{3,2},{4,3},{5,4},{6,5},{7,6},{9,8},{10,9},{11,10},{12... | collective-permute-start | bytes 147464 | tf_op jit(solution)/shard_map/ppermute | solution.py:32
  98.4 18.1 %copy-start.4 = (s32[4]{0:T(128)S(1)}, s32[4]{0:T(128)}, u32[]{:S(2)}) copy-start(s32[4]{0:T(128)} %pad_add_fusion.at_ref) | copy-start | bytes 52
  100.1 6.4 %collective-permute-start.94 = (bf16[192,512]{1,0:T(8,128)(2,1)S(1)}, bf16[192,512]{1,0:T(8,128)(2,1)S(1)}, u32[]{:S(2)}, u32[]{:S(2)}) collective-permute-start(bf16[192,512]{1,0:T(8,128)(2,1)S(1)} %get-tuple-element.278), channel_id=1, source_target_pairs={{0,128},{1,129},{2,130},{3,131},{4,132},{5,133},{6,134},{7,135},{8... | collective-permute-start | bytes 589832 | tf_op jit(solution)/shard_map/ppermute | solution.py:16
  100.6 13.5 %collective-permute-start.95 = (bf16[192,512]{1,0:T(8,128)(2,1)S(1)}, bf16[192,512]{1,0:T(8,128)(2,1)S(1)}, u32[]{:S(2)}, u32[]{:S(2)}) collective-permute-start(bf16[192,512]{1,0:T(8,128)(2,1)S(1)} %get-tuple-element.279), channel_id=1, source_target_pairs={{0,4},{1,5},{2,6},{3,7},{4,0},{5,1},{6,2},{7,3},{8,12},{9,13},{10,... | collective-permute-start | bytes 589832 | tf_op jit(solution)/shard_map/ppermute | solution.py:16
  104.5 11.9 %collective-permute-start.96 = (bf16[192,512]{1,0:T(8,128)(2,1)S(1)}, bf16[192,512]{1,0:T(8,128)(2,1)S(1)}, u32[]{:S(2)}, u32[]{:S(2)}) collective-permute-start(bf16[192,512]{1,0:T(8,128)(2,1)S(1)} %get-tuple-element.280), channel_id=1, source_target_pairs={{0,132},{1,133},{2,134},{3,135},{4,128},{5,129},{6,130},{7,131},{8... | collective-permute-start | bytes 589832 | tf_op jit(solution)/shard_map/ppermute | solution.py:16
  117.1 3.6 %collective-permute-start.97 = (bf16[96,512]{1,0:T(8,128)(2,1)S(1)}, bf16[96,512]{1,0:T(8,128)(2,1)S(1)}, u32[]{:S(2)}, u32[]{:S(2)}) collective-permute-start(bf16[96,512]{1,0:T(8,128)(2,1)S(1)} %get-tuple-element.283), channel_id=1, source_target_pairs={{0,16},{1,17},{2,18},{3,19},{4,20},{5,21},{6,22},{7,23},{8,24},{9,... | collective-permute-start | bytes 294920 | tf_op jit(solution)/shard_map/ppermute | solution.py:16
  117.2 4.5 %collective-permute-start.98 = (bf16[96,512]{1,0:T(8,128)(2,1)S(1)}, bf16[96,512]{1,0:T(8,128)(2,1)S(1)}, u32[]{:S(2)}, u32[]{:S(2)}) collective-permute-start(bf16[96,512]{1,0:T(8,128)(2,1)S(1)} %get-tuple-element.284), channel_id=1, source_target_pairs={{0,32},{1,33},{2,34},{3,35},{4,36},{5,37},{6,38},{7,39},{8,40},{9,... | collective-permute-start | bytes 294920 | tf_op jit(solution)/shard_map/ppermute | solution.py:16
  117.3 11.9 %collective-permute-start.99 = (bf16[96,512]{1,0:T(8,128)(2,1)S(1)}, bf16[96,512]{1,0:T(8,128)(2,1)S(1)}, u32[]{:S(2)}, u32[]{:S(2)}) collective-permute-start(bf16[96,512]{1,0:T(8,128)(2,1)S(1)} %get-tuple-element.285), channel_id=1, source_target_pairs={{0,48},{1,49},{2,50},{3,51},{4,52},{5,53},{6,54},{7,55},{8,56},{9,... | collective-permute-start | bytes 294920 | tf_op jit(solution)/shard_map/ppermute | solution.py:16
  129.3 7.9 %collective-permute-start.50 = (f32[48,512]{1,0:T(8,128)S(1)}, f32[48,512]{1,0:T(8,128)}, u32[]{:S(2)}, u32[]{:S(2)}) collective-permute-start(f32[48,512]{1,0:T(8,128)S(1)} %get-tuple-element.170), channel_id=1, source_target_pairs={{0,96},{1,97},{2,98},{3,99},{4,100},{5,101},{6,102},{7,103},{8,104... | collective-permute-start | bytes 294920 | tf_op jit(solution)/shard_map/cond/branch_1_fun/ppermute | solution.py:16
  129.4 1.3 collective-permute-start.51
  137.2 3.0 %copy-start.7 = (f32[16,22,512]{2,1,0:T(8,128)S(1)}, f32[16,22,512]{2,1,0:T(8,128)}, u32[]{:S(2)}) copy-start(f32[16,22,512]{2,1,0:T(8,128)} %get-tuple-element.303) | copy-start | bytes 2162692
  137.2 3.0 %copy-start.9 = (bf16[16,16,512]{2,1,0:T(8,128)(2,1)S(1)}, bf16[16,16,512]{2,1,0:T(8,128)(2,1)}, u32[]{:S(2)}) copy-start(bf16[16,16,512]{2,1,0:T(8,128)(2,1)} %param.42) | copy-start | bytes 786436
  138.8 2.3 %collective-permute-start.100 = (f32[32,512]{1,0:T(8,128)S(1)}, f32[32,512]{1,0:T(8,128)S(1)}, u32[]{:S(2)}, u32[]{:S(2)}) collective-permute-start(f32[32,512]{1,0:T(8,128)S(1)} %get-tuple-element.294.half_ref), channel_id=1, source_target_pairs={{0,8},{1,9},{2,10},{3,11},{4,12},{5,13},{6,14},{7,15},{8,0},{9,1},... | collective-permute-start | bytes 196616 | tf_op jit(solution)/shard_map/ppermute | solution.py:16
where the time goes:
time: 144 us; the launch traced here: 142 us
  waiting for transfers between devices  57.6 us (40%)
  starting transfers between devices  37.6 us (26%)
  Pallas kernels  28.2 us (20%)
  other arithmetic  11.1 us (8%)
  local copies, waits for them, and re-layouts  4.11 us (3%)
  matrix products  2.06 us (1%)
  between operations  1.61 us (1%)
    ppermute x12, waiting for transfers between devices, send(): return lax.ppermute(value, DEVICES, [(i, i ^ mask) for i in range(256)])  36.9 us
    pallas_call x8, Pallas kernels, local_call(): pl.pallas_call(kernel, out_shape=[jax.ShapeDtypeStruct(s, d) for s, d in...  28.2 us
    ppermute x12, starting transfers between devices, send(): return lax.ppermute(value, DEVICES, [(i, i ^ mask) for i in range(256)])  16.3 us
    ppermute x2, waiting for transfers between devices, to_north(): return lax.ppermute(value, 'lat', [(i, i + 1) for i in range(7)])  12.1 us
    ppermute x2, starting transfers between devices, to_next(): return lax.ppermute(value, 'lon', [(i, (i + 1) % 32) for i in range(32)])  8.21 us
    ppermute x2, waiting for transfers between devices, to_south(): return lax.ppermute(value, 'lat', [(i + 1, i) for i in range(7)])  5.48 us
    ppermute x2, starting transfers between devices, to_north(): return lax.ppermute(value, 'lat', [(i, i + 1) for i in range(7)])  5.31 us
  transfers between devices with their start and end apart: 26, of which 14 were waited for; matrix products, arithmetic and copies ran while one was open for 6% of the time, Pallas kernels for 4%

commit v1 on v0

--- a/solution.py
+++ b/solution.py
@@ -42,12 +42,12 @@
     return lax.ppermute(value, DEVICES, pairs)
 
 
-def mirror_tiles(value, half_turn, others, transfer):
+def mirror_tiles(value, half_turn):
     def branch(k):
         pairs = [(e * 8 + 7, ((2 * k - e) % 32) * 8 + 7) for e in range(32)]
-        return lambda v, *rest: (lax.ppermute(v, DEVICES, pairs), *transfer(*rest))
-
-    return lax.switch(half_turn, [branch(k) for k in range(16)], value, *others)
+        return lambda v: lax.ppermute(v, DEVICES, pairs)
+
+    return lax.switch(half_turn, [branch(k) for k in range(16)], value)
 
 
 ROOT_2_PI = 0.7978845608028654
@@ -427,11 +427,11 @@
     even = (turn & 1) == 0
 
     top_rows = field[:, width_lat - 3 :, :]
-    mine, south, north = mirror_tiles(
-        top_rows, turn >> 1, (top_rows, field[:, 0:3, :]), lambda a, b: (to_north(a), to_south(b))
-    )
-    low = jnp.where(even, top_to_previous(mine), mine)
-    high = jnp.where(even, mine, top_to_next(mine))
+    mine = mirror_tiles(top_rows, turn >> 1)
+    south = to_north(top_rows)
+    north = to_south(field[:, 0:3, :])
+    low = jnp.where(even, to_previous(mine), mine)
+    high = jnp.where(even, mine, to_next(mine))
     fold = lax.dynamic_slice_in_dim(jnp.concatenate([low, high], axis=0), shift, 16, axis=0)
     north = jnp.where(is_north, fold[::-1, ::-1, :], north)
     column = jnp.concatenate([south, field, north], axis=1)
@@ -504,6 +504,8 @@
         room=8,
     )
     taken = [send(piece, mask) for piece, mask in zip(give, Y_MASKS)]
+    from_fold, taken = lax.optimization_barrier((mirror_tiles(mine, turn >> 1), taken))
+    from_fold = from_fold.astype(F32)
 
     own, half, *give = run_sum(
         third_sum_kernel,
@@ -520,12 +522,10 @@
         [own, half, *taken],
         "fourth_sum",
     )
-    from_fold, got = mirror_tiles(mine, turn >> 1, (give,), lambda v: (send(v, Z_MASKS[3]),))
-    from_fold = from_fold.astype(F32)
     grad_down, grad_up, half = run_sum(
         last_sum_kernel,
         [((8, 512), F32), ((2, 2048), F32), ((32, 512), F32)],
-        [keep, half, got],
+        [keep, half, send(give, Z_MASKS[3])],
         "last_sum",
     )
     other = send(half, CORE_MASK)

time: 144 us -> 143 us (level)
  the two profiles are of different devices: /device:TPU:65 before, /device:TPU:7 now
where the time goes in v1:
time: 143 us; the launch traced here: 142 us
  starting transfers between devices  57.9 us (40%)
  waiting for transfers between devices  35.5 us (25%)
  Pallas kernels  27.7 us (19%)
  local copies, waits for them, and re-layouts  8.69 us (6%)
  other arithmetic  8.69 us (6%)
  matrix products  2.09 us (1%)
  between operations  1.6 us (1%)
    pallas_call x8, Pallas kernels, local_call(): pl.pallas_call(kernel, out_shape=[jax.ShapeDtypeStruct(s, d) for s, d in...  27.7 us
    ppermute x12, starting transfers between devices, send(): return lax.ppermute(value, DEVICES, [(i, i ^ mask) for i in range(256)])  24.3 us
    ppermute x2, starting transfers between devices, to_north(): return lax.ppermute(value, 'lat', [(i, i + 1) for i in range(7)])  15.9 us
    ppermute x12, waiting for transfers between devices, send(): return lax.ppermute(value, DEVICES, [(i, i ^ mask) for i in range(256)])  13.7 us
    ppermute x2, waiting for transfers between devices, to_north(): return lax.ppermute(value, 'lat', [(i, i + 1) for i in range(7)])  11.2 us
    ppermute x2, waiting for transfers between devices, to_south(): return lax.ppermute(value, 'lat', [(i + 1, i) for i in range(7)])  9.81 us
    ppermute x3, starting transfers between devices, to_previous(): return lax.ppermute(value, 'lon', [((i + 1) % 32, i) for i in range(32)])  6.1 us
    unnamed x42, local copies, waits for them, and re-layouts  5.65 us
  transfers between devices with their start and end apart: 26, of which 12 were waited for; matrix products, arithmetic and copies ran while one was open for 7% of the time, Pallas kernels for 4%

profile of v1, /device:TPU:7, one launch (start us, length us, event | category | flops | bytes accessed | tf_op | source)
XLA Modules:
  0.0 142.2 jit_solution(11368990192412369066)
XLA Ops:
  0.6 1.3 slice.92
  2.0 1.0 fusion.16
  3.7 1.3 conditional.2
  3.7 1.3 collective-permute-start.13
  5.0 2.2 %collective-permute-start.34 = (bf16[16,3,512]{2,1,0:T(4,128)(2,1)}, bf16[16,3,512]{2,1,0:T(4,128)(2,1)S(1)}, u32[]{:S(2)}, u32[]{:S(2)}) collective-permute-start(bf16[16,3,512]{2,1,0:T(4,128)(2,1)} %get-tuple-element.175), channel_id=1, source_target_pairs={{0,8},{8,16},{16,24},{24,32},{32,40},{40,48},{48,56},{56,64},{64,7... | collective-permute-start | bytes 147464 | tf_op jit(solution)/shard_map/ppermute | solution.py:20
  7.2 4.7 %collective-permute-start.32 = (bf16[16,3,512]{2,1,0:T(4,128)(2,1)S(1)}, bf16[16,3,512]{2,1,0:T(4,128)(2,1)S(1)}, u32[]{:S(2)}, u32[]{:S(2)}) collective-permute-start(bf16[16,3,512]{2,1,0:T(4,128)(2,1)S(1)} %get-tuple-element.170), channel_id=1, source_target_pairs={{0,1},{1,2},{2,3},{3,4},{4,5},{5,6},{6,7},{8,9},{9,10},{10,11},{11... | collective-permute-start | bytes 147464 | tf_op jit(solution)/shard_map/ppermute | solution.py:28
  11.9 1.9 %collective-permute-start.35 = (bf16[16,3,512]{2,1,0:T(4,128)(2,1)S(1)}, bf16[16,3,512]{2,1,0:T(4,128)(2,1)S(1)}, u32[]{:S(2)}, u32[]{:S(2)}) collective-permute-start(bf16[16,3,512]{2,1,0:T(4,128)(2,1)S(1)} %get-tuple-element.169), channel_id=1, source_target_pairs={{1,0},{2,1},{3,2},{4,3},{5,4},{6,5},{7,6},{9,8},{10,9},{11,10},{12... | collective-permute-start | bytes 147464 | tf_op jit(solution)/shard_map/ppermute | solution.py:32
  13.9 0.7 convert_element_type.42
  14.6 0.1 convert_element_type.43
  14.7 1.1 bitcast_multiply_fusion.d_out_ref
  15.7 2.1 %fusion.17.d_act_hbm = f32[256,2048]{1,0:T(8,128)} fusion(bf16[256,512]{1,0:T(8,128)(2,1)S(1)} %bitcast_multiply_fusion.d_out_ref, bf16[2048,512]{1,0:T(8,128)(2,1)S(1)} %copy-done), kind=kOutput, calls=%fused_computation.38 | convolution fusion | flops 536870912 | bytes 4456448 | tf_op jit(solution)/shard_map/dot_general | solution.py:444
  17.8 1.0 fusion.5.order_hbm
  18.8 0.9 broadcast_select_fusion.2
  19.7 0.1 fusion.13
  19.9 0.2 rev.6
  20.1 0.4 collective-permute-done.35
  20.7 6.0 %collective-permute-start.37 = (bf16[3,22,512]{2,1,0:T(8,128)(2,1)S(1)}, bf16[3,22,512]{2,1,0:T(8,128)(2,1)S(1)}, u32[]{:S(2)}, u32[]{:S(2)}) collective-permute-start(bf16[3,22,512]{2,1,0:T(8,128)(2,1)S(1)} %get-tuple-element.168), channel_id=1, source_target_pairs={{8,0},{16,8},{24,16},{32,24},{40,32},{48,40},{56,48},{64,56},{72,6... | collective-permute-start | bytes 202760 | tf_op jit(solution)/shard_map/ppermute | solution.py:24
  26.7 0.7 pad_add_fusion.at_ref
  27.3 0.3 collective-permute-done.37
  27.6 0.5 collective-permute-done.36
  28.1 1.2 fusion.7.ext_ref
  29.3 17.7 %forward.1 = (f32[16,16,512]{2,1,0:T(8,128)}, f32[32,512]{1,0:T(8,128)}, f32[512,512]{1,0:T(8,128)}, bf16[3,512,512]{2,1,0:T(8,128)(2,1)}, bf16[2112,512]{1,0:T(8,128)(2,1)}) custom-call(s32[4]{0:T(128)} %pad_add_fusion.at_ref, bf16[22,32,512]{2,1,0:T(8,128)(2,1)} %fusion.7.ext_ref, f32[49,512]{1,0:T(8,128)} %kern_ref.3, f32[1,512]{1,0:T(1,128)} %bitcast.17, ...), custom_call_target="tpu_custom_call" | custom-call | flops 20000000000 | bytes 2000000 | tf_op jit(solution)/shard_map/forward/pallas_call | solution.py:254
  47.0 4.8 %collective-permute-start.38 = (bf16[2112,512]{1,0:T(8,128)(2,1)}, bf16[2112,512]{1,0:T(8,128)(2,1)S(1)}, u32[]{:S(2)}, u32[]{:S(2)}) collective-permute-start(bf16[2112,512]{1,0:T(8,128)(2,1)} %get-tuple-element.119), channel_id=1, source_target_pairs={{0,8},{1,9},{2,10},{3,11},{4,12},{5,13},{6,14},{7,15},{8,0},{9,1},... | collective-permute-start | bytes 6488072 | tf_op jit(solution)/shard_map/ppermute | solution.py:16
  51.8 1.0 copy-done.12
  52.9 3.8 %rims.1 = (f32[22,24,512]{2,1,0:T(8,128)S(1)}, bf16[3,32,512]{2,1,0:T(8,128)(2,1)S(1)}, bf16[3,32,512]{2,1,0:T(8,128)(2,1)S(1)}) custom-call(f32[16,16,512]{2,1,0:T(8,128)S(1)} %copy-done.12, f32[49,512]{1,0:T(8,128)S(1)} %copy-done.5), custom_call_target="tpu_custom_call" | custom-call | flops 5000000000 | bytes 2000000 | tf_op jit(solution)/shard_map/rims/pallas_call | solution.py:254
  56.7 0.1 collective-permute-start.40
  56.8 1.7 %collective-permute-start.39 = (bf16[3,32,512]{2,1,0:T(8,128)(2,1)S(1)}, bf16[3,32,512]{2,1,0:T(8,128)(2,1)S(1)}, u32[]{:S(2)}, u32[]{:S(2)}) collective-permute-start(bf16[3,32,512]{2,1,0:T(8,128)(2,1)S(1)} %get-tuple-element.122), channel_id=1, source_target_pairs={{0,8},{8,16},{16,24},{24,32},{32,40},{40,48},{48,56},{56,64},{64,7... | collective-permute-start | bytes 294920 | tf_op jit(solution)/shard_map/ppermute | solution.py:20
  58.6 1.4 first_sum.1
  59.9 3.9 %collective-permute-start.47 = (bf16[576,512]{1,0:T(8,128)(2,1)}, bf16[576,512]{1,0:T(8,128)(2,1)}, u32[]{:S(2)}, u32[]{:S(2)}) collective-permute-start(bf16[576,512]{1,0:T(8,128)(2,1)} %get-tuple-element.130), channel_id=1, source_target_pairs={{0,3},{1,2},{2,1},{3,0},{4,7},{5,6},{6,5},{7,4},{8,11},{9,10},{10,... | collective-permute-start | bytes 1769480 | tf_op jit(solution)/shard_map/ppermute | solution.py:16
  63.8 1.0 fusion.14
  64.9 0.2 rev.7
  65.3 0.7 collective-permute-start.42
  66.0 0.7 collective-permute-start.41
  66.7 11.2 %collective-permute-start.43 = (bf16[16,3,512]{2,1,0:T(4,128)(2,1)S(1)}, bf16[16,3,512]{2,1,0:T(4,128)(2,1)S(1)}, u32[]{:S(2)}, u32[]{:S(2)}) collective-permute-start(bf16[16,3,512]{2,1,0:T(4,128)(2,1)S(1)} %get-tuple-element.166), channel_id=1, source_target_pairs={{0,1},{1,2},{2,3},{3,4},{4,5},{5,6},{6,7},{8,9},{9,10},{10,11},{11... | collective-permute-start | bytes 147464 | tf_op jit(solution)/shard_map/ppermute | solution.py:28
  77.9 1.9 %collective-permute-start.44 = (bf16[16,3,512]{2,1,0:T(4,128)(2,1)S(1)}, bf16[16,3,512]{2,1,0:T(4,128)(2,1)S(1)}, u32[]{:S(2)}, u32[]{:S(2)}) collective-permute-start(bf16[16,3,512]{2,1,0:T(4,128)(2,1)S(1)} %get-tuple-element.164), channel_id=1, source_target_pairs={{1,0},{2,1},{3,2},{4,3},{5,4},{6,5},{7,6},{9,8},{10,9},{11,10},{12... | collective-permute-start | bytes 147464 | tf_op jit(solution)/shard_map/ppermute | solution.py:32
  79.9 11.2 %collective-permute-done.43 = bf16[16,3,512]{2,1,0:T(4,128)(2,1)S(1)} collective-permute-done((bf16[16,3,512]{2,1,0:T(4,128)(2,1)S(1)}, bf16[16,3,512]{2,1,0:T(4,128)(2,1)S(1)}, u32[]{:S(2)}, u32[]{:S(2)}) %collective-permute-start.43) | collective-permute-done | bytes 49184 | tf_op jit(solution)/shard_map/ppermute | solution.py:28
  91.1 9.4 %collective-permute-done.44 = bf16[16,3,512]{2,1,0:T(4,128)(2,1)S(1)} collective-permute-done((bf16[16,3,512]{2,1,0:T(4,128)(2,1)S(1)}, bf16[16,3,512]{2,1,0:T(4,128)(2,1)S(1)}, u32[]{:S(2)}, u32[]{:S(2)}) %collective-permute-start.44) | collective-permute-done | bytes 49184 | tf_op jit(solution)/shard_map/ppermute | solution.py:32
  100.5 0.6 copy-done.19
  101.1 0.8 copy-done.7
  102.0 2.2 %second_sum.1 = (f32[128,512]{1,0:T(8,128)S(1)}, f32[32,512]{1,0:T(8,128)S(1)}, bf16[192,512]{1,0:T(8,128)(2,1)}, bf16[192,512]{1,0:T(8,128)(2,1)S(1)}, bf16[192,512]{1,0:T(8,128)(2,1)S(1)}) custom-call(f32[512,512]{1,0:T(8,128)S(1)} %get-tuple-element.134.own_ref, f32[32,512]{1,0:T(8,128)S(1)} %copy-done.7, bf16[576,512]{1,0:T(8,128)(2,1)} %collective-permute-done.45.a_ref, ...), custom_call_target="tpu_custom_call" | custom-call | flops 800000000 | bytes 2000000 | tf_op jit(solution)/shard_map/second_sum/pallas_call | solution.py:254
  104.2 0.7 copy-done.8
  104.9 0.6 copy-done.10
  105.5 3.9 %collective-permute-start.50 = (bf16[192,512]{1,0:T(8,128)(2,1)S(1)}, bf16[192,512]{1,0:T(8,128)(2,1)S(1)}, u32[]{:S(2)}, u32[]{:S(2)}) collective-permute-start(bf16[192,512]{1,0:T(8,128)(2,1)S(1)} %get-tuple-element.141), channel_id=1, source_target_pairs={{0,132},{1,133},{2,134},{3,135},{4,128},{5,129},{6,130},{7,131},{8... | collective-permute-start | bytes 589832 | tf_op jit(solution)/shard_map/ppermute | solution.py:16
  109.4 1.3 conditional.3
  109.4 1.3 collective-permute-start.29
  110.7 1.2 collective-permute-done.48.a_ref
  111.8 2.3 %collective-permute-done.49.b_ref = bf16[192,512]{1,0:T(8,128)(2,1)S(1)} collective-permute-done((bf16[192,512]{1,0:T(8,128)(2,1)S(1)}, bf16[192,512]{1,0:T(8,128)(2,1)S(1)}, u32[]{:S(2)}, u32[]{:S(2)}) %collective-permute-start.49) | collective-permute-done | bytes 196640 | tf_op jit(solution)/shard_map/ppermute | solution.py:16
  114.1 4.4 %collective-permute-done.50.c_ref = bf16[192,512]{1,0:T(8,128)(2,1)S(1)} collective-permute-done((bf16[192,512]{1,0:T(8,128)(2,1)S(1)}, bf16[192,512]{1,0:T(8,128)(2,1)S(1)}, u32[]{:S(2)}, u32[]{:S(2)}) %collective-permute-start.50) | collective-permute-done | bytes 196640 | tf_op jit(solution)/shard_map/ppermute | solution.py:16
  118.5 0.9 copy-done.9
  119.5 0.8 copy-done.11
  120.3 0.7 third_sum.1
  121.0 0.1 collective-permute-start.51
  121.1 1.6 %collective-permute-start.52 = (bf16[96,512]{1,0:T(8,128)(2,1)S(1)}, bf16[96,512]{1,0:T(8,128)(2,1)S(1)}, u32[]{:S(2)}, u32[]{:S(2)}) collective-permute-start(bf16[96,512]{1,0:T(8,128)(2,1)S(1)} %get-tuple-element.151), channel_id=1, source_target_pairs={{0,32},{1,33},{2,34},{3,35},{4,36},{5,37},{6,38},{7,39},{8,40},{9,... | collective-permute-start | bytes 294920 | tf_op jit(solution)/shard_map/ppermute | solution.py:16
  122.7 1.9 %collective-permute-start.53 = (bf16[96,512]{1,0:T(8,128)(2,1)S(1)}, bf16[96,512]{1,0:T(8,128)(2,1)S(1)}, u32[]{:S(2)}, u32[]{:S(2)}) collective-permute-start(bf16[96,512]{1,0:T(8,128)(2,1)S(1)} %get-tuple-element.152), channel_id=1, source_target_pairs={{0,48},{1,49},{2,50},{3,51},{4,52},{5,53},{6,54},{7,55},{8,56},{9,... | collective-permute-start | bytes 294920 | tf_op jit(solution)/shard_map/ppermute | solution.py:16
  124.6 0.3 collective-permute-done.51.a_ref
  124.9 1.1 collective-permute-done.52.b_ref
  126.0 3.4 %collective-permute-done.53.c_ref = bf16[96,512]{1,0:T(8,128)(2,1)S(1)} collective-permute-done((bf16[96,512]{1,0:T(8,128)(2,1)S(1)}, bf16[96,512]{1,0:T(8,128)(2,1)S(1)}, u32[]{:S(2)}, u32[]{:S(2)}) %collective-permute-start.53) | collective-permute-done | bytes 98336 | tf_op jit(solution)/shard_map/ppermute | solution.py:16
  129.4 3.9 %collective-permute-start.54 = (f32[48,512]{1,0:T(8,128)S(1)}, f32[48,512]{1,0:T(8,128)S(1)}, u32[]{:S(2)}, u32[]{:S(2)}) collective-permute-start(f32[48,512]{1,0:T(8,128)S(1)} %get-tuple-element.155), channel_id=1, source_target_pairs={{0,96},{1,97},{2,98},{3,99},{4,100},{5,101},{6,102},{7,103},{8,104... | collective-permute-start | bytes 294920 | tf_op jit(solution)/shard_map/ppermute | solution.py:16
  133.3 0.9 convert_add_fusion.1
  134.2 1.1 collective-permute-done.54.got_ref
  135.3 0.6 last_sum.1
  135.9 4.2 %collective-permute-start.55 = (f32[32,512]{1,0:T(8,128)S(1)}, f32[32,512]{1,0:T(8,128)S(1)}, u32[]{:S(2)}, u32[]{:S(2)}) collective-permute-start(f32[32,512]{1,0:T(8,128)S(1)} %get-tuple-element.158.half_ref), channel_id=1, source_target_pairs={{0,8},{1,9},{2,10},{3,11},{4,12},{5,13},{6,14},{7,15},{8,0},{9,1},... | collective-permute-start | bytes 196616 | tf_op jit(solution)/shard_map/ppermute | solution.py:16
  140.1 0.9 fusion.12
  141.0 1.2 split.1
  (66 shorter events, 0.6 us)
Async XLA Ops:
  0.6 15.1 %copy-start = (bf16[2048,512]{1,0:T(8,128)(2,1)S(1)}, bf16[2048,512]{1,0:T(8,128)(2,1)}, u32[]{:S(2)}) copy-start(bf16[2048,512]{1,0:T(8,128)(2,1)} %param.49) | copy-start | bytes 6291460
  3.7 1.3 collective-permute-start.13
  5.0 13.8 %collective-permute-start.34 = (bf16[16,3,512]{2,1,0:T(4,128)(2,1)}, bf16[16,3,512]{2,1,0:T(4,128)(2,1)S(1)}, u32[]{:S(2)}, u32[]{:S(2)}) collective-permute-start(bf16[16,3,512]{2,1,0:T(4,128)(2,1)} %get-tuple-element.175), channel_id=1, source_target_pairs={{0,8},{8,16},{16,24},{24,32},{32,40},{40,48},{48,56},{56,64},{64,7... | collective-permute-start | bytes 147464 | tf_op jit(solution)/shard_map/ppermute | solution.py:20
  7.2 11.6 %collective-permute-start.33 = (bf16[16,3,512]{2,1,0:T(4,128)(2,1)}, bf16[16,3,512]{2,1,0:T(4,128)(2,1)S(1)}, u32[]{:S(2)}, u32[]{:S(2)}) collective-permute-start(bf16[16,3,512]{2,1,0:T(4,128)(2,1)} %get-tuple-element.175), channel_id=1, source_target_pairs={{8,0},{16,8},{24,16},{32,24},{40,32},{48,40},{56,48},{64,56},{72,6... | collective-permute-start | bytes 147464 | tf_op jit(solution)/shard_map/ppermute | solution.py:24
  7.2 13.4 %collective-permute-start.32 = (bf16[16,3,512]{2,1,0:T(4,128)(2,1)S(1)}, bf16[16,3,512]{2,1,0:T(4,128)(2,1)S(1)}, u32[]{:S(2)}, u32[]{:S(2)}) collective-permute-start(bf16[16,3,512]{2,1,0:T(4,128)(2,1)S(1)} %get-tuple-element.170), channel_id=1, source_target_pairs={{0,1},{1,2},{2,3},{3,4},{4,5},{5,6},{6,7},{8,9},{9,10},{10,11},{11... | collective-permute-start | bytes 147464 | tf_op jit(solution)/shard_map/ppermute | solution.py:28
  11.9 8.6 %collective-permute-start.35 = (bf16[16,3,512]{2,1,0:T(4,128)(2,1)S(1)}, bf16[16,3,512]{2,1,0:T(4,128)(2,1)S(1)}, u32[]{:S(2)}, u32[]{:S(2)}) collective-permute-start(bf16[16,3,512]{2,1,0:T(4,128)(2,1)S(1)} %get-tuple-element.169), channel_id=1, source_target_pairs={{1,0},{2,1},{3,2},{4,3},{5,4},{6,5},{7,6},{9,8},{10,9},{11,10},{12... | collective-permute-start | bytes 147464 | tf_op jit(solution)/shard_map/ppermute | solution.py:32
  15.7 2.1 %copy-start.16 = (bf16[256,512]{1,0:T(8,128)(2,1)}, bf16[256,512]{1,0:T(8,128)(2,1)S(1)}, u32[]{:S(2)}) copy-start(bf16[256,512]{1,0:T(8,128)(2,1)S(1)} %bitcast_multiply_fusion.d_out_ref) | copy-start | bytes 786436
  17.8 2.8 %copy-start.14 = (bf16[16,16,512]{2,1,0:T(8,128)(2,1)S(1)}, bf16[16,16,512]{2,1,0:T(8,128)(2,1)}, u32[]{:S(2)}) copy-start(bf16[16,16,512]{2,1,0:T(8,128)(2,1)} %param.41) | copy-start | bytes 786436
  20.7 6.9 %collective-permute-start.37 = (bf16[3,22,512]{2,1,0:T(8,128)(2,1)S(1)}, bf16[3,22,512]{2,1,0:T(8,128)(2,1)S(1)}, u32[]{:S(2)}, u32[]{:S(2)}) collective-permute-start(bf16[3,22,512]{2,1,0:T(8,128)(2,1)S(1)} %get-tuple-element.168), channel_id=1, source_target_pairs={{8,0},{16,8},{24,16},{32,24},{40,32},{48,40},{56,48},{64,56},{72,6... | collective-permute-start | bytes 202760 | tf_op jit(solution)/shard_map/ppermute | solution.py:24
  26.7 1.4 collective-permute-start.36
  29.3 22.6 %copy-start.5 = (f32[49,512]{1,0:T(8,128)S(1)}, f32[49,512]{1,0:T(8,128)}, u32[]{:S(2)}) copy-start(f32[49,512]{1,0:T(8,128)} %kern_ref.3) | copy-start | bytes 301060
  47.0 9.7 %collective-permute-start.38 = (bf16[2112,512]{1,0:T(8,128)(2,1)}, bf16[2112,512]{1,0:T(8,128)(2,1)S(1)}, u32[]{:S(2)}, u32[]{:S(2)}) collective-permute-start(bf16[2112,512]{1,0:T(8,128)(2,1)} %get-tuple-element.119), channel_id=1, source_target_pairs={{0,8},{1,9},{2,10},{3,11},{4,12},{5,13},{6,14},{7,15},{8,0},{9,1},... | collective-permute-start | bytes 6488072 | tf_op jit(solution)/shard_map/ppermute | solution.py:16
  51.8 1.0 copy-start.12
  52.9 5.7 %copy-start.1 = (bf16[3,512,512]{2,1,0:T(8,128)(2,1)S(1)}, bf16[3,512,512]{2,1,0:T(8,128)(2,1)}, u32[]{:S(2)}) copy-start(bf16[3,512,512]{2,1,0:T(8,128)(2,1)} %get-tuple-element.125.keep_ref) | copy-start | bytes 4718596
  52.9 5.7 %copy-start.2 = (f32[512,512]{1,0:T(8,128)S(1)}, f32[512,512]{1,0:T(8,128)}, u32[]{:S(2)}) copy-start(f32[512,512]{1,0:T(8,128)} %get-tuple-element.124.mine_ref) | copy-start | bytes 3145732
  52.9 5.7 %copy-start.3 = (f32[32,512]{1,0:T(8,128)S(1)}, f32[32,512]{1,0:T(8,128)}, u32[]{:S(2)}) copy-start(f32[32,512]{1,0:T(8,128)} %get-tuple-element.127.half_ref) | copy-start | bytes 196612
  56.7 7.1 %collective-permute-start.40 = (bf16[3,32,512]{2,1,0:T(8,128)(2,1)S(1)}, bf16[3,32,512]{2,1,0:T(8,128)(2,1)S(1)}, u32[]{:S(2)}, u32[]{:S(2)}) collective-permute-start(bf16[3,32,512]{2,1,0:T(8,128)(2,1)S(1)} %get-tuple-element.123), channel_id=1, source_target_pairs={{8,0},{16,8},{24,16},{32,24},{40,32},{48,40},{56,48},{64,56},{72,6... | collective-permute-start | bytes 294920 | tf_op jit(solution)/shard_map/ppermute | solution.py:24
  56.8 7.0 %collective-permute-start.39 = (bf16[3,32,512]{2,1,0:T(8,128)(2,1)S(1)}, bf16[3,32,512]{2,1,0:T(8,128)(2,1)S(1)}, u32[]{:S(2)}, u32[]{:S(2)}) collective-permute-start(bf16[3,32,512]{2,1,0:T(8,128)(2,1)S(1)} %get-tuple-element.122), channel_id=1, source_target_pairs={{0,8},{8,16},{16,24},{24,32},{32,40},{40,48},{48,56},{56,64},{64,7... | collective-permute-start | bytes 294920 | tf_op jit(solution)/shard_map/ppermute | solution.py:20
  59.9 4.9 %copy-start.6 = (f32[32,512]{1,0:T(8,128)}, f32[32,512]{1,0:T(8,128)S(1)}, u32[]{:S(2)}) copy-start(f32[32,512]{1,0:T(8,128)S(1)} %get-tuple-element.135.terms_ref) | copy-start | bytes 196612
  59.9 40.6 %collective-permute-start.45 = (bf16[576,512]{1,0:T(8,128)(2,1)}, bf16[576,512]{1,0:T(8,128)(2,1)}, u32[]{:S(2)}, u32[]{:S(2)}) collective-permute-start(bf16[576,512]{1,0:T(8,128)(2,1)} %get-tuple-element.128), channel_id=1, source_target_pairs={{0,1},{1,0},{2,3},{3,2},{4,5},{5,4},{6,7},{7,6},{8,9},{9,8},{10,11... | collective-permute-start | bytes 1769480 | tf_op jit(solution)/shard_map/ppermute | solution.py:16
  59.9 40.6 %collective-permute-start.46 = (bf16[576,512]{1,0:T(8,128)(2,1)}, bf16[576,512]{1,0:T(8,128)(2,1)}, u32[]{:S(2)}, u32[]{:S(2)}) collective-permute-start(bf16[576,512]{1,0:T(8,128)(2,1)} %get-tuple-element.129), channel_id=1, source_target_pairs={{0,2},{1,3},{2,0},{3,1},{4,6},{5,7},{6,4},{7,5},{8,10},{9,11},{10,... | collective-permute-start | bytes 1769480 | tf_op jit(solution)/shard_map/ppermute | solution.py:16
  59.9 40.6 %collective-permute-start.47 = (bf16[576,512]{1,0:T(8,128)(2,1)}, bf16[576,512]{1,0:T(8,128)(2,1)}, u32[]{:S(2)}, u32[]{:S(2)}) collective-permute-start(bf16[576,512]{1,0:T(8,128)(2,1)} %get-tuple-element.130), channel_id=1, source_target_pairs={{0,3},{1,2},{2,1},{3,0},{4,7},{5,6},{6,5},{7,4},{8,11},{9,10},{10,... | collective-permute-start | bytes 1769480 | tf_op jit(solution)/shard_map/ppermute | solution.py:16
  65.3 1.3 collective-permute-start.42
  66.0 11.9 %collective-permute-start.41 = (bf16[16,3,512]{2,1,0:T(4,128)(2,1)S(1)}, bf16[16,3,512]{2,1,0:T(4,128)(2,1)S(1)}, u32[]{:S(2)}, u32[]{:S(2)}) collective-permute-start(bf16[16,3,512]{2,1,0:T(4,128)(2,1)S(1)} %get-tuple-element.171), channel_id=1, source_target_pairs={{7,15},{15,23},{23,31},{31,39},{39,47},{47,55},{55,63},{63,71},{71... | collective-permute-start | bytes 147464 | tf_op jit(solution)/shard_map/ppermute | solution.py:37
  66.7 24.4 %collective-permute-start.43 = (bf16[16,3,512]{2,1,0:T(4,128)(2,1)S(1)}, bf16[16,3,512]{2,1,0:T(4,128)(2,1)S(1)}, u32[]{:S(2)}, u32[]{:S(2)}) collective-permute-start(bf16[16,3,512]{2,1,0:T(4,128)(2,1)S(1)} %get-tuple-element.166), channel_id=1, source_target_pairs={{0,1},{1,2},{2,3},{3,4},{4,5},{5,6},{6,7},{8,9},{9,10},{10,11},{11... | collective-permute-start | bytes 147464 | tf_op jit(solution)/shard_map/ppermute | solution.py:28
  77.9 22.6 %collective-permute-start.44 = (bf16[16,3,512]{2,1,0:T(4,128)(2,1)S(1)}, bf16[16,3,512]{2,1,0:T(4,128)(2,1)S(1)}, u32[]{:S(2)}, u32[]{:S(2)}) collective-permute-start(bf16[16,3,512]{2,1,0:T(4,128)(2,1)S(1)} %get-tuple-element.164), channel_id=1, source_target_pairs={{1,0},{2,1},{3,2},{4,3},{5,4},{6,5},{7,6},{9,8},{10,9},{11,10},{12... | collective-permute-start | bytes 147464 | tf_op jit(solution)/shard_map/ppermute | solution.py:32
  91.1 9.4 %copy-start.17 = (bf16[16,3,512]{2,1,0:T(4,128)(2,1)}, bf16[16,3,512]{2,1,0:T(4,128)(2,1)S(1)}, u32[]{:S(2)}) copy-start(bf16[16,3,512]{2,1,0:T(4,128)(2,1)S(1)} %collective-permute-done.43) | copy-start | bytes 147460
  100.5 0.6 copy-start.19
  101.1 0.8 copy-start.7
  102.0 16.5 %copy-start.4 = (s32[4]{0:T(128)S(1)}, s32[4]{0:T(128)}, u32[]{:S(2)}) copy-start(s32[4]{0:T(128)} %pad_add_fusion.at_ref) | copy-start | bytes 52
  104.2 0.7 copy-start.8
  104.9 0.6 copy-start.10
  105.5 6.3 %collective-permute-start.48 = (bf16[192,512]{1,0:T(8,128)(2,1)}, bf16[192,512]{1,0:T(8,128)(2,1)S(1)}, u32[]{:S(2)}, u32[]{:S(2)}) collective-permute-start(bf16[192,512]{1,0:T(8,128)(2,1)} %get-tuple-element.139), channel_id=1, source_target_pairs={{0,128},{1,129},{2,130},{3,131},{4,132},{5,133},{6,134},{7,135},{8... | collective-permute-start | bytes 589832 | tf_op jit(solution)/shard_map/ppermute | solution.py:16
  105.5 8.6 %collective-permute-start.49 = (bf16[192,512]{1,0:T(8,128)(2,1)S(1)}, bf16[192,512]{1,0:T(8,128)(2,1)S(1)}, u32[]{:S(2)}, u32[]{:S(2)}) collective-permute-start(bf16[192,512]{1,0:T(8,128)(2,1)S(1)} %get-tuple-element.140), channel_id=1, source_target_pairs={{0,4},{1,5},{2,6},{3,7},{4,0},{5,1},{6,2},{7,3},{8,12},{9,13},{10,... | collective-permute-start | bytes 589832 | tf_op jit(solution)/shard_map/ppermute | solution.py:16
  105.5 13.0 %collective-permute-start.50 = (bf16[192,512]{1,0:T(8,128)(2,1)S(1)}, bf16[192,512]{1,0:T(8,128)(2,1)S(1)}, u32[]{:S(2)}, u32[]{:S(2)}) collective-permute-start(bf16[192,512]{1,0:T(8,128)(2,1)S(1)} %get-tuple-element.141), channel_id=1, source_target_pairs={{0,132},{1,133},{2,134},{3,135},{4,128},{5,129},{6,130},{7,131},{8... | collective-permute-start | bytes 589832 | tf_op jit(solution)/shard_map/ppermute | solution.py:16
  109.4 1.3 collective-permute-start.29
  118.5 1.0 copy-start.9
  119.5 0.8 copy-start.11
  121.0 3.9 %collective-permute-start.51 = (bf16[96,512]{1,0:T(8,128)(2,1)S(1)}, bf16[96,512]{1,0:T(8,128)(2,1)S(1)}, u32[]{:S(2)}, u32[]{:S(2)}) collective-permute-start(bf16[96,512]{1,0:T(8,128)(2,1)S(1)} %get-tuple-element.150), channel_id=1, source_target_pairs={{0,16},{1,17},{2,18},{3,19},{4,20},{5,21},{6,22},{7,23},{8,24},{9,... | collective-permute-start | bytes 294920 | tf_op jit(solution)/shard_map/ppermute | solution.py:16
  121.1 4.9 %collective-permute-start.52 = (bf16[96,512]{1,0:T(8,128)(2,1)S(1)}, bf16[96,512]{1,0:T(8,128)(2,1)S(1)}, u32[]{:S(2)}, u32[]{:S(2)}) collective-permute-start(bf16[96,512]{1,0:T(8,128)(2,1)S(1)} %get-tuple-element.151), channel_id=1, source_target_pairs={{0,32},{1,33},{2,34},{3,35},{4,36},{5,37},{6,38},{7,39},{8,40},{9,... | collective-permute-start | bytes 294920 | tf_op jit(solution)/shard_map/ppermute | solution.py:16
  122.7 6.6 %collective-permute-start.53 = (bf16[96,512]{1,0:T(8,128)(2,1)S(1)}, bf16[96,512]{1,0:T(8,128)(2,1)S(1)}, u32[]{:S(2)}, u32[]{:S(2)}) collective-permute-start(bf16[96,512]{1,0:T(8,128)(2,1)S(1)} %get-tuple-element.152), channel_id=1, source_target_pairs={{0,48},{1,49},{2,50},{3,51},{4,52},{5,53},{6,54},{7,55},{8,56},{9,... | collective-permute-start | bytes 294920 | tf_op jit(solution)/shard_map/ppermute | solution.py:16
  129.4 3.9 %copy-start.20 = (bf16[16,3,512]{2,1,0:T(4,128)(2,1)S(1)}, bf16[16,3,512]{2,1,0:T(4,128)(2,1)}, u32[]{:S(2)}) copy-start(bf16[16,3,512]{2,1,0:T(4,128)(2,1)} %copy-done.19) | copy-start | bytes 147460
  129.4 5.9 %collective-permute-start.54 = (f32[48,512]{1,0:T(8,128)S(1)}, f32[48,512]{1,0:T(8,128)S(1)}, u32[]{:S(2)}, u32[]{:S(2)}) collective-permute-start(f32[48,512]{1,0:T(8,128)S(1)} %get-tuple-element.155), channel_id=1, source_target_pairs={{0,96},{1,97},{2,98},{3,99},{4,100},{5,101},{6,102},{7,103},{8,104... | collective-permute-start | bytes 294920 | tf_op jit(solution)/shard_map/ppermute | solution.py:16
  135.3 4.8 %copy-start.13 = (f32[16,22,512]{2,1,0:T(8,128)S(1)}, f32[16,22,512]{2,1,0:T(8,128)}, u32[]{:S(2)}) copy-start(f32[16,22,512]{2,1,0:T(8,128)} %get-tuple-element.163) | copy-start | bytes 2162692
  135.3 4.8 %copy-start.15 = (bf16[16,16,512]{2,1,0:T(8,128)(2,1)S(1)}, bf16[16,16,512]{2,1,0:T(8,128)(2,1)}, u32[]{:S(2)}) copy-start(bf16[16,16,512]{2,1,0:T(8,128)(2,1)} %param.42) | copy-start | bytes 786436
  135.3 4.8 %copy-start.18 = (bf16[16,3,512]{2,1,0:T(4,128)(2,1)S(1)}, bf16[16,3,512]{2,1,0:T(4,128)(2,1)}, u32[]{:S(2)}) copy-start(bf16[16,3,512]{2,1,0:T(4,128)(2,1)} %copy-done.17) | copy-start | bytes 147460
  135.9 5.1 %collective-permute-start.55 = (f32[32,512]{1,0:T(8,128)S(1)}, f32[32,512]{1,0:T(8,128)S(1)}, u32[]{:S(2)}, u32[]{:S(2)}) collective-permute-start(f32[32,512]{1,0:T(8,128)S(1)} %get-tuple-element.158.half_ref), channel_id=1, source_target_pairs={{0,8},{1,9},{2,10},{3,11},{4,12},{5,13},{6,14},{7,15},{8,0},{9,1},... | collective-permute-start | bytes 196616 | tf_op jit(solution)/shard_map/ppermute | solution.py:16

commit v2 on v1

--- a/solution.py
+++ b/solution.py
@@ -101,7 +101,7 @@
         normed[rows, :] = (center * lax.rsqrt(spread + 1e-6) * gain_ref[...]).astype(BF16)
         return carry
 
-    lax.fori_loop(0, 8, norm_step, 0)
+    lax.fori_loop(0, 8, norm_step, 0, unroll=8)
     for load in loads:
         load.wait()
     ordered[...] = jnp.dot(normed[...], order_ref[...], preferred_element_type=F32).astype(BF16)
@@ -122,7 +122,7 @@
             d_upper_ref[rows, lanes] = d_up
             return bias + jnp.sum(d_up.astype(F32), axis=0, keepdims=True)
 
-        small_ref[50 + t : 51 + t, :] = lax.fori_loop(0, 8, gelu_step, jnp.zeros((1, 512), F32))
+        small_ref[50 + t : 51 + t, :] = lax.fori_loop(0, 8, gelu_step, jnp.zeros((1, 512), F32), unroll=4)
         tile[...] = lax.dot_general(
             active[...], d_out_ref[...], (((0,), (0,)), ((), ())), preferred_element_type=F32
         )
@@ -184,7 +184,7 @@
         d_cells[pl.ds(step * 2, 2)] = d_mixed.reshape(2, 16, 512)
         return gain_sum + jnp.sum(d * unit, axis=0, keepdims=True)
 
-    small_ref[49:50, :] = lax.fori_loop(0, 8, norm_step, jnp.zeros((1, 512), F32))
+    small_ref[49:50, :] = lax.fori_loop(0, 8, norm_step, jnp.zeros((1, 512), F32), unroll=8)
     small_ref[54:64, :] = jnp.zeros((10, 512), F32)
     stores.append(pltpu.make_async_copy(d_cells, d_cells_hbm, sems.at[7]))
     stores[-1].start()

time: 143 us -> 140 us (0.979)
  Pallas kernels: 27.7 us -> 23.8 us
    pallas_call x8, Pallas kernels: 27.7 us -> 23.8 us  [local_call(): pl.pallas_call(kernel, out_shape=[jax.ShapeDtypeStruct(s, d) for s, d in...]
where the time goes in v2:
time: 140 us; the launch traced here: 138 us
  starting transfers between devices  56.6 us (40%)
  waiting for transfers between devices  36.4 us (26%)
  Pallas kernels  23.8 us (17%)
  local copies, waits for them, and re-layouts  8.69 us (6%)
  other arithmetic  8.69 us (6%)
  matrix products  2.09 us (1%)
  between operations  1.6 us (1%)
    pallas_call x8, Pallas kernels, local_call(): pl.pallas_call(kernel, out_shape=[jax.ShapeDtypeStruct(s, d) for s, d in...  23.8 us
    ppermute x12, starting transfers between devices, send(): return lax.ppermute(value, DEVICES, [(i, i ^ mask) for i in range(256)])  23.4 us
    ppermute x2, starting transfers between devices, to_north(): return lax.ppermute(value, 'lat', [(i, i + 1) for i in range(7)])  15.5 us
    ppermute x12, waiting for transfers between devices, send(): return lax.ppermute(value, DEVICES, [(i, i ^ mask) for i in range(256)])  14.6 us
    ppermute x2, waiting for transfers between devices, to_north(): return lax.ppermute(value, 'lat', [(i, i + 1) for i in range(7)])  11.7 us
    ppermute x2, waiting for transfers between devices, to_south(): return lax.ppermute(value, 'lat', [(i + 1, i) for i in range(7)])  9.34 us
    ppermute x3, starting transfers between devices, to_previous(): return lax.ppermute(value, 'lon', [((i + 1) % 32, i) for i in range(32)])  6.1 us
    unnamed x42, local copies, waits for them, and re-layouts  5.65 us
  transfers between devices with their start and end apart: 26, of which 12 were waited for; matrix products, arithmetic and copies ran while one was open for 7% of the time, Pallas kernels for 4%

profile of v2, /device:TPU:7, one launch (start us, length us, event | category | flops | bytes accessed | tf_op | source)
XLA Modules:
  0.0 137.9 jit_solution(298637193199178207)
XLA Ops:
  0.6 1.3 slice.92
  2.0 1.0 fusion.16
  3.7 1.3 conditional.2
  3.7 1.3 collective-permute-start.12
  5.0 2.2 %collective-permute-start.34 = (bf16[16,3,512]{2,1,0:T(4,128)(2,1)}, bf16[16,3,512]{2,1,0:T(4,128)(2,1)S(1)}, u32[]{:S(2)}, u32[]{:S(2)}) collective-permute-start(bf16[16,3,512]{2,1,0:T(4,128)(2,1)} %get-tuple-element.175), channel_id=1, source_target_pairs={{0,8},{8,16},{16,24},{24,32},{32,40},{40,48},{48,56},{56,64},{64,7... | collective-permute-start | bytes 147464 | tf_op jit(solution)/shard_map/ppermute | solution.py:20
  7.2 4.7 %collective-permute-start.32 = (bf16[16,3,512]{2,1,0:T(4,128)(2,1)S(1)}, bf16[16,3,512]{2,1,0:T(4,128)(2,1)S(1)}, u32[]{:S(2)}, u32[]{:S(2)}) collective-permute-start(bf16[16,3,512]{2,1,0:T(4,128)(2,1)S(1)} %get-tuple-element.170), channel_id=1, source_target_pairs={{0,1},{1,2},{2,3},{3,4},{4,5},{5,6},{6,7},{8,9},{9,10},{10,11},{11... | collective-permute-start | bytes 147464 | tf_op jit(solution)/shard_map/ppermute | solution.py:28
  11.9 1.9 %collective-permute-start.35 = (bf16[16,3,512]{2,1,0:T(4,128)(2,1)S(1)}, bf16[16,3,512]{2,1,0:T(4,128)(2,1)S(1)}, u32[]{:S(2)}, u32[]{:S(2)}) collective-permute-start(bf16[16,3,512]{2,1,0:T(4,128)(2,1)S(1)} %get-tuple-element.169), channel_id=1, source_target_pairs={{1,0},{2,1},{3,2},{4,3},{5,4},{6,5},{7,6},{9,8},{10,9},{11,10},{12... | collective-permute-start | bytes 147464 | tf_op jit(solution)/shard_map/ppermute | solution.py:32
  13.9 0.7 convert_element_type.42
  14.6 0.1 convert_element_type.43
  14.7 1.1 bitcast_multiply_fusion.d_out_ref
  15.7 2.1 %fusion.17.d_act_hbm = f32[256,2048]{1,0:T(8,128)} fusion(bf16[256,512]{1,0:T(8,128)(2,1)S(1)} %bitcast_multiply_fusion.d_out_ref, bf16[2048,512]{1,0:T(8,128)(2,1)S(1)} %copy-done), kind=kOutput, calls=%fused_computation.38 | convolution fusion | flops 536870912 | bytes 4456448 | tf_op jit(solution)/shard_map/dot_general | solution.py:444
  17.8 1.0 fusion.5.order_hbm
  18.8 0.9 broadcast_select_fusion.2
  19.7 0.1 fusion.13
  19.9 0.2 rev.6
  20.1 0.4 collective-permute-done.35
  20.7 6.0 %collective-permute-start.37 = (bf16[3,22,512]{2,1,0:T(8,128)(2,1)S(1)}, bf16[3,22,512]{2,1,0:T(8,128)(2,1)S(1)}, u32[]{:S(2)}, u32[]{:S(2)}) collective-permute-start(bf16[3,22,512]{2,1,0:T(8,128)(2,1)S(1)} %get-tuple-element.168), channel_id=1, source_target_pairs={{8,0},{16,8},{24,16},{32,24},{40,32},{48,40},{56,48},{64,56},{72,6... | collective-permute-start | bytes 202760 | tf_op jit(solution)/shard_map/ppermute | solution.py:24
  26.7 0.7 pad_add_fusion.at_ref
  27.3 0.3 collective-permute-done.37
  27.6 0.5 collective-permute-done.36
  28.1 1.2 fusion.7.ext_ref
  29.3 13.9 %forward.1 = (f32[16,16,512]{2,1,0:T(8,128)}, f32[32,512]{1,0:T(8,128)}, f32[512,512]{1,0:T(8,128)}, bf16[3,512,512]{2,1,0:T(8,128)(2,1)}, bf16[2112,512]{1,0:T(8,128)(2,1)}) custom-call(s32[4]{0:T(128)} %pad_add_fusion.at_ref, bf16[22,32,512]{2,1,0:T(8,128)(2,1)} %fusion.7.ext_ref, f32[49,512]{1,0:T(8,128)} %kern_ref.3, f32[1,512]{1,0:T(1,128)} %bitcast.17, ...), custom_call_target="tpu_custom_call" | custom-call | flops 20000000000 | bytes 2000000 | tf_op jit(solution)/shard_map/forward/pallas_call | solution.py:254
  43.2 4.8 %collective-permute-start.38 = (bf16[2112,512]{1,0:T(8,128)(2,1)}, bf16[2112,512]{1,0:T(8,128)(2,1)S(1)}, u32[]{:S(2)}, u32[]{:S(2)}) collective-permute-start(bf16[2112,512]{1,0:T(8,128)(2,1)} %get-tuple-element.119), channel_id=1, source_target_pairs={{0,8},{1,9},{2,10},{3,11},{4,12},{5,13},{6,14},{7,15},{8,0},{9,1},... | collective-permute-start | bytes 6488072 | tf_op jit(solution)/shard_map/ppermute | solution.py:16
  48.0 1.0 copy-done.12
  49.1 3.8 %rims.1 = (f32[22,24,512]{2,1,0:T(8,128)S(1)}, bf16[3,32,512]{2,1,0:T(8,128)(2,1)S(1)}, bf16[3,32,512]{2,1,0:T(8,128)(2,1)S(1)}) custom-call(f32[16,16,512]{2,1,0:T(8,128)S(1)} %copy-done.12, f32[49,512]{1,0:T(8,128)S(1)} %copy-done.5), custom_call_target="tpu_custom_call" | custom-call | flops 5000000000 | bytes 2000000 | tf_op jit(solution)/shard_map/rims/pallas_call | solution.py:254
  52.9 0.1 collective-permute-start.40
  53.0 1.7 %collective-permute-start.39 = (bf16[3,32,512]{2,1,0:T(8,128)(2,1)S(1)}, bf16[3,32,512]{2,1,0:T(8,128)(2,1)S(1)}, u32[]{:S(2)}, u32[]{:S(2)}) collective-permute-start(bf16[3,32,512]{2,1,0:T(8,128)(2,1)S(1)} %get-tuple-element.122), channel_id=1, source_target_pairs={{0,8},{8,16},{16,24},{24,32},{32,40},{40,48},{48,56},{56,64},{64,7... | collective-permute-start | bytes 294920 | tf_op jit(solution)/shard_map/ppermute | solution.py:20
  54.7 1.4 first_sum.1
  56.1 3.9 %collective-permute-start.47 = (bf16[576,512]{1,0:T(8,128)(2,1)}, bf16[576,512]{1,0:T(8,128)(2,1)}, u32[]{:S(2)}, u32[]{:S(2)}) collective-permute-start(bf16[576,512]{1,0:T(8,128)(2,1)} %get-tuple-element.130), channel_id=1, source_target_pairs={{0,3},{1,2},{2,1},{3,0},{4,7},{5,6},{6,5},{7,4},{8,11},{9,10},{10,... | collective-permute-start | bytes 1769480 | tf_op jit(solution)/shard_map/ppermute | solution.py:16
  60.0 1.0 fusion.14
  61.1 0.2 rev.7
  61.5 0.7 collective-permute-start.42
  62.2 0.7 collective-permute-start.41
  62.9 10.7 %collective-permute-start.43 = (bf16[16,3,512]{2,1,0:T(4,128)(2,1)S(1)}, bf16[16,3,512]{2,1,0:T(4,128)(2,1)S(1)}, u32[]{:S(2)}, u32[]{:S(2)}) collective-permute-start(bf16[16,3,512]{2,1,0:T(4,128)(2,1)S(1)} %get-tuple-element.166), channel_id=1, source_target_pairs={{0,1},{1,2},{2,3},{3,4},{4,5},{5,6},{6,7},{8,9},{9,10},{10,11},{11... | collective-permute-start | bytes 147464 | tf_op jit(solution)/shard_map/ppermute | solution.py:28
  73.6 1.9 %collective-permute-start.44 = (bf16[16,3,512]{2,1,0:T(4,128)(2,1)S(1)}, bf16[16,3,512]{2,1,0:T(4,128)(2,1)S(1)}, u32[]{:S(2)}, u32[]{:S(2)}) collective-permute-start(bf16[16,3,512]{2,1,0:T(4,128)(2,1)S(1)} %get-tuple-element.164), channel_id=1, source_target_pairs={{1,0},{2,1},{3,2},{4,3},{5,4},{6,5},{7,6},{9,8},{10,9},{11,10},{12... | collective-permute-start | bytes 147464 | tf_op jit(solution)/shard_map/ppermute | solution.py:32
  75.6 11.7 %collective-permute-done.43 = bf16[16,3,512]{2,1,0:T(4,128)(2,1)S(1)} collective-permute-done((bf16[16,3,512]{2,1,0:T(4,128)(2,1)S(1)}, bf16[16,3,512]{2,1,0:T(4,128)(2,1)S(1)}, u32[]{:S(2)}, u32[]{:S(2)}) %collective-permute-start.43) | collective-permute-done | bytes 49184 | tf_op jit(solution)/shard_map/ppermute | solution.py:28
  87.3 8.9 %collective-permute-done.44 = bf16[16,3,512]{2,1,0:T(4,128)(2,1)S(1)} collective-permute-done((bf16[16,3,512]{2,1,0:T(4,128)(2,1)S(1)}, bf16[16,3,512]{2,1,0:T(4,128)(2,1)S(1)}, u32[]{:S(2)}, u32[]{:S(2)}) %collective-permute-start.44) | collective-permute-done | bytes 49184 | tf_op jit(solution)/shard_map/ppermute | solution.py:32
  96.3 0.6 copy-done.19
  96.9 0.8 copy-done.7
  97.7 2.2 %second_sum.1 = (f32[128,512]{1,0:T(8,128)S(1)}, f32[32,512]{1,0:T(8,128)S(1)}, bf16[192,512]{1,0:T(8,128)(2,1)}, bf16[192,512]{1,0:T(8,128)(2,1)S(1)}, bf16[192,512]{1,0:T(8,128)(2,1)S(1)}) custom-call(f32[512,512]{1,0:T(8,128)S(1)} %get-tuple-element.134.own_ref, f32[32,512]{1,0:T(8,128)S(1)} %copy-done.7, bf16[576,512]{1,0:T(8,128)(2,1)} %collective-permute-done.45.a_ref, ...), custom_call_target="tpu_custom_call" | custom-call | flops 800000000 | bytes 2000000 | tf_op jit(solution)/shard_map/second_sum/pallas_call | solution.py:254
  99.9 0.7 copy-done.8
  100.6 0.6 copy-done.10
  101.2 3.9 %collective-permute-start.50 = (bf16[192,512]{1,0:T(8,128)(2,1)S(1)}, bf16[192,512]{1,0:T(8,128)(2,1)S(1)}, u32[]{:S(2)}, u32[]{:S(2)}) collective-permute-start(bf16[192,512]{1,0:T(8,128)(2,1)S(1)} %get-tuple-element.141), channel_id=1, source_target_pairs={{0,132},{1,133},{2,134},{3,135},{4,128},{5,129},{6,130},{7,131},{8... | collective-permute-start | bytes 589832 | tf_op jit(solution)/shard_map/ppermute | solution.py:16
  105.1 1.3 conditional.3
  105.1 1.3 collective-permute-start.28
  106.4 1.2 collective-permute-done.48.a_ref
  107.5 2.3 %collective-permute-done.49.b_ref = bf16[192,512]{1,0:T(8,128)(2,1)S(1)} collective-permute-done((bf16[192,512]{1,0:T(8,128)(2,1)S(1)}, bf16[192,512]{1,0:T(8,128)(2,1)S(1)}, u32[]{:S(2)}, u32[]{:S(2)}) %collective-permute-start.49) | collective-permute-done | bytes 196640 | tf_op jit(solution)/shard_map/ppermute | solution.py:16
  109.8 4.4 %collective-permute-done.50.c_ref = bf16[192,512]{1,0:T(8,128)(2,1)S(1)} collective-permute-done((bf16[192,512]{1,0:T(8,128)(2,1)S(1)}, bf16[192,512]{1,0:T(8,128)(2,1)S(1)}, u32[]{:S(2)}, u32[]{:S(2)}) %collective-permute-start.50) | collective-permute-done | bytes 196640 | tf_op jit(solution)/shard_map/ppermute | solution.py:16
  114.2 0.9 copy-done.9
  115.2 0.8 copy-done.11
  116.0 0.7 third_sum.1
  116.7 0.1 collective-permute-start.51
  116.8 2.6 %collective-permute-start.52 = (bf16[96,512]{1,0:T(8,128)(2,1)S(1)}, bf16[96,512]{1,0:T(8,128)(2,1)S(1)}, u32[]{:S(2)}, u32[]{:S(2)}) collective-permute-start(bf16[96,512]{1,0:T(8,128)(2,1)S(1)} %get-tuple-element.151), channel_id=1, source_target_pairs={{0,32},{1,33},{2,34},{3,35},{4,36},{5,37},{6,38},{7,39},{8,40},{9,... | collective-permute-start | bytes 294920 | tf_op jit(solution)/shard_map/ppermute | solution.py:16
  119.4 1.0 collective-permute-start.53
  120.3 0.3 collective-permute-done.51.a_ref
  120.6 1.3 collective-permute-done.52.b_ref
  121.9 4.0 %collective-permute-done.53.c_ref = bf16[96,512]{1,0:T(8,128)(2,1)S(1)} collective-permute-done((bf16[96,512]{1,0:T(8,128)(2,1)S(1)}, bf16[96,512]{1,0:T(8,128)(2,1)S(1)}, u32[]{:S(2)}, u32[]{:S(2)}) %collective-permute-start.53) | collective-permute-done | bytes 98336 | tf_op jit(solution)/shard_map/ppermute | solution.py:16
  126.0 4.0 %collective-permute-start.54 = (f32[48,512]{1,0:T(8,128)S(1)}, f32[48,512]{1,0:T(8,128)S(1)}, u32[]{:S(2)}, u32[]{:S(2)}) collective-permute-start(f32[48,512]{1,0:T(8,128)S(1)} %get-tuple-element.155), channel_id=1, source_target_pairs={{0,96},{1,97},{2,98},{3,99},{4,100},{5,101},{6,102},{7,103},{8,104... | collective-permute-start | bytes 294920 | tf_op jit(solution)/shard_map/ppermute | solution.py:16
  130.0 0.9 convert_add_fusion.1
  130.9 1.1 collective-permute-done.54.got_ref
  132.1 0.6 last_sum.1
  132.7 3.2 %collective-permute-start.55 = (f32[32,512]{1,0:T(8,128)S(1)}, f32[32,512]{1,0:T(8,128)S(1)}, u32[]{:S(2)}, u32[]{:S(2)}) collective-permute-start(f32[32,512]{1,0:T(8,128)S(1)} %get-tuple-element.158.half_ref), channel_id=1, source_target_pairs={{0,8},{1,9},{2,10},{3,11},{4,12},{5,13},{6,14},{7,15},{8,0},{9,1},... | collective-permute-start | bytes 196616 | tf_op jit(solution)/shard_map/ppermute | solution.py:16
  135.8 0.9 fusion.12
  136.7 1.2 split.1
  (66 shorter events, 0.6 us)
Async XLA Ops:
  0.6 15.1 %copy-start = (bf16[2048,512]{1,0:T(8,128)(2,1)S(1)}, bf16[2048,512]{1,0:T(8,128)(2,1)}, u32[]{:S(2)}) copy-start(bf16[2048,512]{1,0:T(8,128)(2,1)} %param.49) | copy-start | bytes 6291460
  3.7 1.3 collective-permute-start.12
  5.0 13.8 %collective-permute-start.34 = (bf16[16,3,512]{2,1,0:T(4,128)(2,1)}, bf16[16,3,512]{2,1,0:T(4,128)(2,1)S(1)}, u32[]{:S(2)}, u32[]{:S(2)}) collective-permute-start(bf16[16,3,512]{2,1,0:T(4,128)(2,1)} %get-tuple-element.175), channel_id=1, source_target_pairs={{0,8},{8,16},{16,24},{24,32},{32,40},{40,48},{48,56},{56,64},{64,7... | collective-permute-start | bytes 147464 | tf_op jit(solution)/shard_map/ppermute | solution.py:20
  7.2 11.7 %collective-permute-start.33 = (bf16[16,3,512]{2,1,0:T(4,128)(2,1)}, bf16[16,3,512]{2,1,0:T(4,128)(2,1)S(1)}, u32[]{:S(2)}, u32[]{:S(2)}) collective-permute-start(bf16[16,3,512]{2,1,0:T(4,128)(2,1)} %get-tuple-element.175), channel_id=1, source_target_pairs={{8,0},{16,8},{24,16},{32,24},{40,32},{48,40},{56,48},{64,56},{72,6... | collective-permute-start | bytes 147464 | tf_op jit(solution)/shard_map/ppermute | solution.py:24
  7.2 13.4 %collective-permute-start.32 = (bf16[16,3,512]{2,1,0:T(4,128)(2,1)S(1)}, bf16[16,3,512]{2,1,0:T(4,128)(2,1)S(1)}, u32[]{:S(2)}, u32[]{:S(2)}) collective-permute-start(bf16[16,3,512]{2,1,0:T(4,128)(2,1)S(1)} %get-tuple-element.170), channel_id=1, source_target_pairs={{0,1},{1,2},{2,3},{3,4},{4,5},{5,6},{6,7},{8,9},{9,10},{10,11},{11... | collective-permute-start | bytes 147464 | tf_op jit(solution)/shard_map/ppermute | solution.py:28
  11.9 8.6 %collective-permute-start.35 = (bf16[16,3,512]{2,1,0:T(4,128)(2,1)S(1)}, bf16[16,3,512]{2,1,0:T(4,128)(2,1)S(1)}, u32[]{:S(2)}, u32[]{:S(2)}) collective-permute-start(bf16[16,3,512]{2,1,0:T(4,128)(2,1)S(1)} %get-tuple-element.169), channel_id=1, source_target_pairs={{1,0},{2,1},{3,2},{4,3},{5,4},{6,5},{7,6},{9,8},{10,9},{11,10},{12... | collective-permute-start | bytes 147464 | tf_op jit(solution)/shard_map/ppermute | solution.py:32
  15.7 2.1 %copy-start.16 = (bf16[256,512]{1,0:T(8,128)(2,1)}, bf16[256,512]{1,0:T(8,128)(2,1)S(1)}, u32[]{:S(2)}) copy-start(bf16[256,512]{1,0:T(8,128)(2,1)S(1)} %bitcast_multiply_fusion.d_out_ref) | copy-start | bytes 786436
  17.8 2.8 %copy-start.14 = (bf16[16,16,512]{2,1,0:T(8,128)(2,1)S(1)}, bf16[16,16,512]{2,1,0:T(8,128)(2,1)}, u32[]{:S(2)}) copy-start(bf16[16,16,512]{2,1,0:T(8,128)(2,1)} %param.41) | copy-start | bytes 786436
  20.7 6.9 %collective-permute-start.37 = (bf16[3,22,512]{2,1,0:T(8,128)(2,1)S(1)}, bf16[3,22,512]{2,1,0:T(8,128)(2,1)S(1)}, u32[]{:S(2)}, u32[]{:S(2)}) collective-permute-start(bf16[3,22,512]{2,1,0:T(8,128)(2,1)S(1)} %get-tuple-element.168), channel_id=1, source_target_pairs={{8,0},{16,8},{24,16},{32,24},{40,32},{48,40},{56,48},{64,56},{72,6... | collective-permute-start | bytes 202760 | tf_op jit(solution)/shard_map/ppermute | solution.py:24
  26.7 1.4 %collective-permute-start.36 = (bf16[3,22,512]{2,1,0:T(8,128)(2,1)S(1)}, bf16[3,22,512]{2,1,0:T(8,128)(2,1)S(1)}, u32[]{:S(2)}, u32[]{:S(2)}) collective-permute-start(bf16[3,22,512]{2,1,0:T(8,128)(2,1)S(1)} %get-tuple-element.167), channel_id=1, source_target_pairs={{0,8},{8,16},{16,24},{24,32},{32,40},{40,48},{48,56},{56,64},{64,7... | collective-permute-start | bytes 202760 | tf_op jit(solution)/shard_map/ppermute | solution.py:20
  29.3 18.7 %copy-start.5 = (f32[49,512]{1,0:T(8,128)S(1)}, f32[49,512]{1,0:T(8,128)}, u32[]{:S(2)}) copy-start(f32[49,512]{1,0:T(8,128)} %kern_ref.3) | copy-start | bytes 301060
  43.2 9.7 %collective-permute-start.38 = (bf16[2112,512]{1,0:T(8,128)(2,1)}, bf16[2112,512]{1,0:T(8,128)(2,1)S(1)}, u32[]{:S(2)}, u32[]{:S(2)}) collective-permute-start(bf16[2112,512]{1,0:T(8,128)(2,1)} %get-tuple-element.119), channel_id=1, source_target_pairs={{0,8},{1,9},{2,10},{3,11},{4,12},{5,13},{6,14},{7,15},{8,0},{9,1},... | collective-permute-start | bytes 6488072 | tf_op jit(solution)/shard_map/ppermute | solution.py:16
  48.0 1.0 copy-start.12
  49.1 5.7 %copy-start.1 = (bf16[3,512,512]{2,1,0:T(8,128)(2,1)S(1)}, bf16[3,512,512]{2,1,0:T(8,128)(2,1)}, u32[]{:S(2)}) copy-start(bf16[3,512,512]{2,1,0:T(8,128)(2,1)} %get-tuple-element.125.keep_ref) | copy-start | bytes 4718596
  49.1 5.7 %copy-start.2 = (f32[512,512]{1,0:T(8,128)S(1)}, f32[512,512]{1,0:T(8,128)}, u32[]{:S(2)}) copy-start(f32[512,512]{1,0:T(8,128)} %get-tuple-element.124.mine_ref) | copy-start | bytes 3145732
  49.1 5.7 %copy-start.3 = (f32[32,512]{1,0:T(8,128)S(1)}, f32[32,512]{1,0:T(8,128)}, u32[]{:S(2)}) copy-start(f32[32,512]{1,0:T(8,128)} %get-tuple-element.127.half_ref) | copy-start | bytes 196612
  52.9 7.1 %collective-permute-start.40 = (bf16[3,32,512]{2,1,0:T(8,128)(2,1)S(1)}, bf16[3,32,512]{2,1,0:T(8,128)(2,1)S(1)}, u32[]{:S(2)}, u32[]{:S(2)}) collective-permute-start(bf16[3,32,512]{2,1,0:T(8,128)(2,1)S(1)} %get-tuple-element.123), channel_id=1, source_target_pairs={{8,0},{16,8},{24,16},{32,24},{40,32},{48,40},{56,48},{64,56},{72,6... | collective-permute-start | bytes 294920 | tf_op jit(solution)/shard_map/ppermute | solution.py:24
  53.0 7.0 %collective-permute-start.39 = (bf16[3,32,512]{2,1,0:T(8,128)(2,1)S(1)}, bf16[3,32,512]{2,1,0:T(8,128)(2,1)S(1)}, u32[]{:S(2)}, u32[]{:S(2)}) collective-permute-start(bf16[3,32,512]{2,1,0:T(8,128)(2,1)S(1)} %get-tuple-element.122), channel_id=1, source_target_pairs={{0,8},{8,16},{16,24},{24,32},{32,40},{40,48},{48,56},{56,64},{64,7... | collective-permute-start | bytes 294920 | tf_op jit(solution)/shard_map/ppermute | solution.py:20
  56.1 4.9 %copy-start.6 = (f32[32,512]{1,0:T(8,128)}, f32[32,512]{1,0:T(8,128)S(1)}, u32[]{:S(2)}) copy-start(f32[32,512]{1,0:T(8,128)S(1)} %get-tuple-element.135.terms_ref) | copy-start | bytes 196612
  56.1 40.1 %collective-permute-start.45 = (bf16[576,512]{1,0:T(8,128)(2,1)}, bf16[576,512]{1,0:T(8,128)(2,1)}, u32[]{:S(2)}, u32[]{:S(2)}) collective-permute-start(bf16[576,512]{1,0:T(8,128)(2,1)} %get-tuple-element.128), channel_id=1, source_target_pairs={{0,1},{1,0},{2,3},{3,2},{4,5},{5,4},{6,7},{7,6},{8,9},{9,8},{10,11... | collective-permute-start | bytes 1769480 | tf_op jit(solution)/shard_map/ppermute | solution.py:16
  56.1 40.1 %collective-permute-start.46 = (bf16[576,512]{1,0:T(8,128)(2,1)}, bf16[576,512]{1,0:T(8,128)(2,1)}, u32[]{:S(2)}, u32[]{:S(2)}) collective-permute-start(bf16[576,512]{1,0:T(8,128)(2,1)} %get-tuple-element.129), channel_id=1, source_target_pairs={{0,2},{1,3},{2,0},{3,1},{4,6},{5,7},{6,4},{7,5},{8,10},{9,11},{10,... | collective-permute-start | bytes 1769480 | tf_op jit(solution)/shard_map/ppermute | solution.py:16
  56.1 40.1 %collective-permute-start.47 = (bf16[576,512]{1,0:T(8,128)(2,1)}, bf16[576,512]{1,0:T(8,128)(2,1)}, u32[]{:S(2)}, u32[]{:S(2)}) collective-permute-start(bf16[576,512]{1,0:T(8,128)(2,1)} %get-tuple-element.130), channel_id=1, source_target_pairs={{0,3},{1,2},{2,1},{3,0},{4,7},{5,6},{6,5},{7,4},{8,11},{9,10},{10,... | collective-permute-start | bytes 1769480 | tf_op jit(solution)/shard_map/ppermute | solution.py:16
  61.5 1.3 collective-permute-start.42
  62.2 11.4 %collective-permute-start.41 = (bf16[16,3,512]{2,1,0:T(4,128)(2,1)S(1)}, bf16[16,3,512]{2,1,0:T(4,128)(2,1)S(1)}, u32[]{:S(2)}, u32[]{:S(2)}) collective-permute-start(bf16[16,3,512]{2,1,0:T(4,128)(2,1)S(1)} %get-tuple-element.171), channel_id=1, source_target_pairs={{7,15},{15,23},{23,31},{31,39},{39,47},{47,55},{55,63},{63,71},{71... | collective-permute-start | bytes 147464 | tf_op jit(solution)/shard_map/ppermute | solution.py:37
  62.9 24.4 %collective-permute-start.43 = (bf16[16,3,512]{2,1,0:T(4,128)(2,1)S(1)}, bf16[16,3,512]{2,1,0:T(4,128)(2,1)S(1)}, u32[]{:S(2)}, u32[]{:S(2)}) collective-permute-start(bf16[16,3,512]{2,1,0:T(4,128)(2,1)S(1)} %get-tuple-element.166), channel_id=1, source_target_pairs={{0,1},{1,2},{2,3},{3,4},{4,5},{5,6},{6,7},{8,9},{9,10},{10,11},{11... | collective-permute-start | bytes 147464 | tf_op jit(solution)/shard_map/ppermute | solution.py:28
  73.6 22.6 %collective-permute-start.44 = (bf16[16,3,512]{2,1,0:T(4,128)(2,1)S(1)}, bf16[16,3,512]{2,1,0:T(4,128)(2,1)S(1)}, u32[]{:S(2)}, u32[]{:S(2)}) collective-permute-start(bf16[16,3,512]{2,1,0:T(4,128)(2,1)S(1)} %get-tuple-element.164), channel_id=1, source_target_pairs={{1,0},{2,1},{3,2},{4,3},{5,4},{6,5},{7,6},{9,8},{10,9},{11,10},{12... | collective-permute-start | bytes 147464 | tf_op jit(solution)/shard_map/ppermute | solution.py:32
  87.3 8.9 %copy-start.17 = (bf16[16,3,512]{2,1,0:T(4,128)(2,1)}, bf16[16,3,512]{2,1,0:T(4,128)(2,1)S(1)}, u32[]{:S(2)}) copy-start(bf16[16,3,512]{2,1,0:T(4,128)(2,1)S(1)} %collective-permute-done.43) | copy-start | bytes 147460
  96.2 0.6 copy-start.19
  96.8 0.8 copy-start.7
  97.7 16.5 %copy-start.4 = (s32[4]{0:T(128)S(1)}, s32[4]{0:T(128)}, u32[]{:S(2)}) copy-start(s32[4]{0:T(128)} %pad_add_fusion.at_ref) | copy-start | bytes 52
  99.9 0.7 copy-start.8
  100.6 0.6 copy-start.10
  101.2 6.3 %collective-permute-start.48 = (bf16[192,512]{1,0:T(8,128)(2,1)}, bf16[192,512]{1,0:T(8,128)(2,1)S(1)}, u32[]{:S(2)}, u32[]{:S(2)}) collective-permute-start(bf16[192,512]{1,0:T(8,128)(2,1)} %get-tuple-element.139), channel_id=1, source_target_pairs={{0,128},{1,129},{2,130},{3,131},{4,132},{5,133},{6,134},{7,135},{8... | collective-permute-start | bytes 589832 | tf_op jit(solution)/shard_map/ppermute | solution.py:16
  101.2 8.6 %collective-permute-start.49 = (bf16[192,512]{1,0:T(8,128)(2,1)S(1)}, bf16[192,512]{1,0:T(8,128)(2,1)S(1)}, u32[]{:S(2)}, u32[]{:S(2)}) collective-permute-start(bf16[192,512]{1,0:T(8,128)(2,1)S(1)} %get-tuple-element.140), channel_id=1, source_target_pairs={{0,4},{1,5},{2,6},{3,7},{4,0},{5,1},{6,2},{7,3},{8,12},{9,13},{10,... | collective-permute-start | bytes 589832 | tf_op jit(solution)/shard_map/ppermute | solution.py:16
  101.2 13.0 %collective-permute-start.50 = (bf16[192,512]{1,0:T(8,128)(2,1)S(1)}, bf16[192,512]{1,0:T(8,128)(2,1)S(1)}, u32[]{:S(2)}, u32[]{:S(2)}) collective-permute-start(bf16[192,512]{1,0:T(8,128)(2,1)S(1)} %get-tuple-element.141), channel_id=1, source_target_pairs={{0,132},{1,133},{2,134},{3,135},{4,128},{5,129},{6,130},{7,131},{8... | collective-permute-start | bytes 589832 | tf_op jit(solution)/shard_map/ppermute | solution.py:16
  105.1 1.3 collective-permute-start.28
  114.2 1.0 copy-start.9
  115.2 0.8 copy-start.11
  116.7 3.9 %collective-permute-start.51 = (bf16[96,512]{1,0:T(8,128)(2,1)S(1)}, bf16[96,512]{1,0:T(8,128)(2,1)S(1)}, u32[]{:S(2)}, u32[]{:S(2)}) collective-permute-start(bf16[96,512]{1,0:T(8,128)(2,1)S(1)} %get-tuple-element.150), channel_id=1, source_target_pairs={{0,16},{1,17},{2,18},{3,19},{4,20},{5,21},{6,22},{7,23},{8,24},{9,... | collective-permute-start | bytes 294920 | tf_op jit(solution)/shard_map/ppermute | solution.py:16
  116.8 5.1 %collective-permute-start.52 = (bf16[96,512]{1,0:T(8,128)(2,1)S(1)}, bf16[96,512]{1,0:T(8,128)(2,1)S(1)}, u32[]{:S(2)}, u32[]{:S(2)}) collective-permute-start(bf16[96,512]{1,0:T(8,128)(2,1)S(1)} %get-tuple-element.151), channel_id=1, source_target_pairs={{0,32},{1,33},{2,34},{3,35},{4,36},{5,37},{6,38},{7,39},{8,40},{9,... | collective-permute-start | bytes 294920 | tf_op jit(solution)/shard_map/ppermute | solution.py:16
  119.4 6.6 %collective-permute-start.53 = (bf16[96,512]{1,0:T(8,128)(2,1)S(1)}, bf16[96,512]{1,0:T(8,128)(2,1)S(1)}, u32[]{:S(2)}, u32[]{:S(2)}) collective-permute-start(bf16[96,512]{1,0:T(8,128)(2,1)S(1)} %get-tuple-element.152), channel_id=1, source_target_pairs={{0,48},{1,49},{2,50},{3,51},{4,52},{5,53},{6,54},{7,55},{8,56},{9,... | collective-permute-start | bytes 294920 | tf_op jit(solution)/shard_map/ppermute | solution.py:16
  125.9 4.1 %copy-start.20 = (bf16[16,3,512]{2,1,0:T(4,128)(2,1)S(1)}, bf16[16,3,512]{2,1,0:T(4,128)(2,1)}, u32[]{:S(2)}) copy-start(bf16[16,3,512]{2,1,0:T(4,128)(2,1)} %copy-done.19) | copy-start | bytes 147460
  126.0 6.1 %collective-permute-start.54 = (f32[48,512]{1,0:T(8,128)S(1)}, f32[48,512]{1,0:T(8,128)S(1)}, u32[]{:S(2)}, u32[]{:S(2)}) collective-permute-start(f32[48,512]{1,0:T(8,128)S(1)} %get-tuple-element.155), channel_id=1, source_target_pairs={{0,96},{1,97},{2,98},{3,99},{4,100},{5,101},{6,102},{7,103},{8,104... | collective-permute-start | bytes 294920 | tf_op jit(solution)/shard_map/ppermute | solution.py:16
  132.0 3.8 %copy-start.13 = (f32[16,22,512]{2,1,0:T(8,128)S(1)}, f32[16,22,512]{2,1,0:T(8,128)}, u32[]{:S(2)}) copy-start(f32[16,22,512]{2,1,0:T(8,128)} %get-tuple-element.163) | copy-start | bytes 2162692
  132.0 3.8 %copy-start.15 = (bf16[16,16,512]{2,1,0:T(8,128)(2,1)S(1)}, bf16[16,16,512]{2,1,0:T(8,128)(2,1)}, u32[]{:S(2)}) copy-start(bf16[16,16,512]{2,1,0:T(8,128)(2,1)} %param.42) | copy-start | bytes 786436
  132.0 3.8 %copy-start.18 = (bf16[16,3,512]{2,1,0:T(4,128)(2,1)S(1)}, bf16[16,3,512]{2,1,0:T(4,128)(2,1)}, u32[]{:S(2)}) copy-start(bf16[16,3,512]{2,1,0:T(4,128)(2,1)} %copy-done.17) | copy-start | bytes 147460
  132.7 4.1 %collective-permute-start.55 = (f32[32,512]{1,0:T(8,128)S(1)}, f32[32,512]{1,0:T(8,128)S(1)}, u32[]{:S(2)}, u32[]{:S(2)}) collective-permute-start(f32[32,512]{1,0:T(8,128)S(1)} %get-tuple-element.158.half_ref), channel_id=1, source_target_pairs={{0,8},{1,9},{2,10},{3,11},{4,12},{5,13},{6,14},{7,15},{8,0},{9,1},... | collective-permute-start | bytes 196616 | tf_op jit(solution)/shard_map/ppermute | solution.py:16

commit v3 on v2

--- a/solution.py
+++ b/solution.py
@@ -501,7 +501,7 @@
         [((128, 512), F32), ((32, 512), F32)] + [((192, 512), BF16)] * 3,
         [own, terms, *taken],
         "second_sum",
-        room=8,
+        room=56,
     )
     taken = [send(piece, mask) for piece, mask in zip(give, Y_MASKS)]
     from_fold, taken = lax.optimization_barrier((mirror_tiles(mine, turn >> 1), taken))
@@ -514,6 +514,7 @@
         "third_sum",
         scalars=1,
         scratch=[((8, 16, 512), F32)],
+        room=56,
     )
     taken = [send(piece, mask) for piece, mask in zip(give, Z_MASKS[:3])]
     keep, half, give = run_sum(

time: 140 us -> 139 us (level)
  Pallas kernels: 23.8 us -> 25.5 us
  local copies, waits for them, and re-layouts: 8.69 us -> 7.1 us
    pallas_call x8, Pallas kernels: 23.8 us -> 25.5 us  [local_call(): pl.pallas_call(kernel, out_shape=[jax.ShapeDtypeStruct(s, d) for s, d in...]
    ppermute x12, starting transfers between devices: 23.4 us -> 25 us  [send(): return lax.ppermute(value, DEVICES, [(i, i ^ mask) for i in range(256)])]
    unnamed x42 -> x40, local copies, waits for them, and re-layouts: 5.65 us -> 4.06 us
    ppermute x12, waiting for transfers between devices: 14.6 us -> 13.1 us  [send(): return lax.ppermute(value, DEVICES, [(i, i ^ mask) for i in range(256)])]
where the time goes in v3:
time: 139 us; the launch traced here: 137 us
  starting transfers between devices  57.1 us (41%)
  waiting for transfers between devices  35.3 us (25%)
  Pallas kernels  25.5 us (18%)
  other arithmetic  8.69 us (6%)
  local copies, waits for them, and re-layouts  7.1 us (5%)
  matrix products  2.09 us (2%)
  between operations  1.6 us (1%)
    pallas_call x8, Pallas kernels, local_call(): pl.pallas_call(kernel, out_shape=[jax.ShapeDtypeStruct(s, d) for s, d in...  25.5 us
    ppermute x12, starting transfers between devices, send(): return lax.ppermute(value, DEVICES, [(i, i ^ mask) for i in range(256)])  25 us
    ppermute x2, starting transfers between devices, to_north(): return lax.ppermute(value, 'lat', [(i, i + 1) for i in range(7)])  14.6 us
    ppermute x12, waiting for transfers between devices, send(): return lax.ppermute(value, DEVICES, [(i, i ^ mask) for i in range(256)])  13.1 us
    ppermute x2, waiting for transfers between devices, to_north(): return lax.ppermute(value, 'lat', [(i, i + 1) for i in range(7)])  12.3 us
    ppermute x2, waiting for transfers between devices, to_south(): return lax.ppermute(value, 'lat', [(i + 1, i) for i in range(7)])  9.19 us
    ppermute x3, starting transfers between devices, to_previous(): return lax.ppermute(value, 'lon', [((i + 1) % 32, i) for i in range(32)])  5.85 us
    unnamed x40, local copies, waits for them, and re-layouts  4.06 us
  transfers between devices with their start and end apart: 26, of which 12 were waited for; matrix products, arithmetic and copies ran while one was open for 7% of the time, Pallas kernels for 4%

profile of v3, /device:TPU:7, one launch (start us, length us, event | category | flops | bytes accessed | tf_op | source)
XLA Modules:
  0.0 137.4 jit_solution(15351997858575594205)
XLA Ops:
  0.6 1.3 slice.92
  2.0 1.0 fusion.16
  3.7 1.3 conditional.2
  3.7 1.3 collective-permute-start
  5.0 2.2 %collective-permute-start.34 = (bf16[16,3,512]{2,1,0:T(4,128)(2,1)}, bf16[16,3,512]{2,1,0:T(4,128)(2,1)S(1)}, u32[]{:S(2)}, u32[]{:S(2)}) collective-permute-start(bf16[16,3,512]{2,1,0:T(4,128)(2,1)} %get-tuple-element.175), channel_id=1, source_target_pairs={{0,8},{8,16},{16,24},{24,32},{32,40},{40,48},{48,56},{56,64},{64,7... | collective-permute-start | bytes 147464 | tf_op jit(solution)/shard_map/ppermute | solution.py:20
  7.2 4.7 %collective-permute-start.32 = (bf16[16,3,512]{2,1,0:T(4,128)(2,1)S(1)}, bf16[16,3,512]{2,1,0:T(4,128)(2,1)S(1)}, u32[]{:S(2)}, u32[]{:S(2)}) collective-permute-start(bf16[16,3,512]{2,1,0:T(4,128)(2,1)S(1)} %get-tuple-element.170), channel_id=1, source_target_pairs={{0,1},{1,2},{2,3},{3,4},{4,5},{5,6},{6,7},{8,9},{9,10},{10,11},{11... | collective-permute-start | bytes 147464 | tf_op jit(solution)/shard_map/ppermute | solution.py:28
  11.9 1.9 %collective-permute-start.35 = (bf16[16,3,512]{2,1,0:T(4,128)(2,1)S(1)}, bf16[16,3,512]{2,1,0:T(4,128)(2,1)S(1)}, u32[]{:S(2)}, u32[]{:S(2)}) collective-permute-start(bf16[16,3,512]{2,1,0:T(4,128)(2,1)S(1)} %get-tuple-element.169), channel_id=1, source_target_pairs={{1,0},{2,1},{3,2},{4,3},{5,4},{6,5},{7,6},{9,8},{10,9},{11,10},{12... | collective-permute-start | bytes 147464 | tf_op jit(solution)/shard_map/ppermute | solution.py:32
  13.8 0.7 convert_element_type.42
  14.5 0.1 convert_element_type.43
  14.6 1.1 bitcast_multiply_fusion.d_out_ref
  15.7 2.1 %fusion.17.d_act_hbm = f32[256,2048]{1,0:T(8,128)} fusion(bf16[256,512]{1,0:T(8,128)(2,1)S(1)} %bitcast_multiply_fusion.d_out_ref, bf16[2048,512]{1,0:T(8,128)(2,1)S(1)} %copy-done), kind=kOutput, calls=%fused_computation.38 | convolution fusion | flops 536870912 | bytes 4456448 | tf_op jit(solution)/shard_map/dot_general | solution.py:444
  17.8 1.0 fusion.5.order_hbm
  18.8 0.9 broadcast_select_fusion.2
  19.7 0.1 fusion.13
  19.9 0.2 rev.6
  20.1 0.7 collective-permute-done.35
  20.8 0.1 pad_maximum_fusion.2
  20.9 5.8 %collective-permute-start.37 = (bf16[3,22,512]{2,1,0:T(8,128)(2,1)S(1)}, bf16[3,22,512]{2,1,0:T(8,128)(2,1)S(1)}, u32[]{:S(2)}, u32[]{:S(2)}) collective-permute-start(bf16[3,22,512]{2,1,0:T(8,128)(2,1)S(1)} %get-tuple-element.168), channel_id=1, source_target_pairs={{8,0},{16,8},{24,16},{32,24},{40,32},{48,40},{56,48},{64,56},{72,6... | collective-permute-start | bytes 202760 | tf_op jit(solution)/shard_map/ppermute | solution.py:24
  26.7 0.6 pad_add_fusion.at_ref
  27.3 0.3 collective-permute-done.37
  27.6 0.5 collective-permute-done.36
  28.1 1.2 fusion.7.ext_ref
  29.3 13.9 %forward.1 = (f32[16,16,512]{2,1,0:T(8,128)}, f32[32,512]{1,0:T(8,128)}, f32[512,512]{1,0:T(8,128)}, bf16[3,512,512]{2,1,0:T(8,128)(2,1)}, bf16[2112,512]{1,0:T(8,128)(2,1)}) custom-call(s32[4]{0:T(128)} %pad_add_fusion.at_ref, bf16[22,32,512]{2,1,0:T(8,128)(2,1)} %fusion.7.ext_ref, f32[49,512]{1,0:T(8,128)} %kern_ref.3, f32[1,512]{1,0:T(1,128)} %bitcast.17, ...), custom_call_target="tpu_custom_call" | custom-call | flops 20000000000 | bytes 2000000 | tf_op jit(solution)/shard_map/forward/pallas_call | solution.py:254
  43.2 4.8 %collective-permute-start.38 = (bf16[2112,512]{1,0:T(8,128)(2,1)}, bf16[2112,512]{1,0:T(8,128)(2,1)S(1)}, u32[]{:S(2)}, u32[]{:S(2)}) collective-permute-start(bf16[2112,512]{1,0:T(8,128)(2,1)} %get-tuple-element.119), channel_id=1, source_target_pairs={{0,8},{1,9},{2,10},{3,11},{4,12},{5,13},{6,14},{7,15},{8,0},{9,1},... | collective-permute-start | bytes 6488072 | tf_op jit(solution)/shard_map/ppermute | solution.py:16
  48.0 1.0 copy-done.10
  49.1 3.8 %rims.1 = (f32[22,24,512]{2,1,0:T(8,128)S(1)}, bf16[3,32,512]{2,1,0:T(8,128)(2,1)S(1)}, bf16[3,32,512]{2,1,0:T(8,128)(2,1)S(1)}) custom-call(f32[16,16,512]{2,1,0:T(8,128)S(1)} %copy-done.10, f32[49,512]{1,0:T(8,128)S(1)} %copy-done.6), custom_call_target="tpu_custom_call" | custom-call | flops 5000000000 | bytes 2000000 | tf_op jit(solution)/shard_map/rims/pallas_call | solution.py:254
  52.9 0.1 collective-permute-start.40
  53.0 1.7 %collective-permute-start.39 = (bf16[3,32,512]{2,1,0:T(8,128)(2,1)S(1)}, bf16[3,32,512]{2,1,0:T(8,128)(2,1)S(1)}, u32[]{:S(2)}, u32[]{:S(2)}) collective-permute-start(bf16[3,32,512]{2,1,0:T(8,128)(2,1)S(1)} %get-tuple-element.122), channel_id=1, source_target_pairs={{0,8},{8,16},{16,24},{24,32},{32,40},{40,48},{48,56},{56,64},{64,7... | collective-permute-start | bytes 294920 | tf_op jit(solution)/shard_map/ppermute | solution.py:20
  54.7 1.0 first_sum.1
  55.8 3.8 %collective-permute-start.47 = (bf16[576,512]{1,0:T(8,128)(2,1)S(1)}, bf16[576,512]{1,0:T(8,128)(2,1)}, u32[]{:S(2)}, u32[]{:S(2)}) collective-permute-start(bf16[576,512]{1,0:T(8,128)(2,1)S(1)} %get-tuple-element.130), channel_id=1, source_target_pairs={{0,3},{1,2},{2,1},{3,0},{4,7},{5,6},{6,5},{7,4},{8,11},{9,10},{10,... | collective-permute-start | bytes 1769480 | tf_op jit(solution)/shard_map/ppermute | solution.py:16
  59.7 1.0 fusion.14
  60.7 0.1 fusion.15
  60.8 0.2 rev.7
  61.2 0.7 collective-permute-start.42
  61.9 0.7 collective-permute-start.41
  62.5 9.9 %collective-permute-start.43 = (bf16[16,3,512]{2,1,0:T(4,128)(2,1)S(1)}, bf16[16,3,512]{2,1,0:T(4,128)(2,1)S(1)}, u32[]{:S(2)}, u32[]{:S(2)}) collective-permute-start(bf16[16,3,512]{2,1,0:T(4,128)(2,1)S(1)} %get-tuple-element.166), channel_id=1, source_target_pairs={{0,1},{1,2},{2,3},{3,4},{4,5},{5,6},{6,7},{8,9},{9,10},{10,11},{11... | collective-permute-start | bytes 147464 | tf_op jit(solution)/shard_map/ppermute | solution.py:28
  72.5 1.9 %collective-permute-start.44 = (bf16[16,3,512]{2,1,0:T(4,128)(2,1)S(1)}, bf16[16,3,512]{2,1,0:T(4,128)(2,1)S(1)}, u32[]{:S(2)}, u32[]{:S(2)}) collective-permute-start(bf16[16,3,512]{2,1,0:T(4,128)(2,1)S(1)} %get-tuple-element.164), channel_id=1, source_target_pairs={{1,0},{2,1},{3,2},{4,3},{5,4},{6,5},{7,6},{9,8},{10,9},{11,10},{12... | collective-permute-start | bytes 147464 | tf_op jit(solution)/shard_map/ppermute | solution.py:32
  74.4 0.1 add_add_fusion
  74.5 12.3 %collective-permute-done.43 = bf16[16,3,512]{2,1,0:T(4,128)(2,1)S(1)} collective-permute-done((bf16[16,3,512]{2,1,0:T(4,128)(2,1)S(1)}, bf16[16,3,512]{2,1,0:T(4,128)(2,1)S(1)}, u32[]{:S(2)}, u32[]{:S(2)}) %collective-permute-start.43) | collective-permute-done | bytes 49184 | tf_op jit(solution)/shard_map/ppermute | solution.py:28
  86.8 8.5 %collective-permute-done.44 = bf16[16,3,512]{2,1,0:T(4,128)(2,1)S(1)} collective-permute-done((bf16[16,3,512]{2,1,0:T(4,128)(2,1)S(1)}, bf16[16,3,512]{2,1,0:T(4,128)(2,1)S(1)}, u32[]{:S(2)}, u32[]{:S(2)}) %collective-permute-start.44) | collective-permute-done | bytes 49184 | tf_op jit(solution)/shard_map/ppermute | solution.py:32
  95.3 0.6 copy-done.15
  95.9 2.8 %second_sum.1 = (f32[128,512]{1,0:T(8,128)}, f32[32,512]{1,0:T(8,128)}, bf16[192,512]{1,0:T(8,128)(2,1)}, bf16[192,512]{1,0:T(8,128)(2,1)}, bf16[192,512]{1,0:T(8,128)(2,1)}) custom-call(f32[512,512]{1,0:T(8,128)} %copy-done.5, f32[32,512]{1,0:T(8,128)} %copy-done.7, bf16[576,512]{1,0:T(8,128)(2,1)} %collective-permute-done.45.a_ref, ...), custom_call_target="tpu_custom_call" | custom-call | flops 800000000 | bytes 2000000 | tf_op jit(solution)/shard_map/second_sum/pallas_call | solution.py:254
  98.7 3.8 %collective-permute-start.50 = (bf16[192,512]{1,0:T(8,128)(2,1)}, bf16[192,512]{1,0:T(8,128)(2,1)S(1)}, u32[]{:S(2)}, u32[]{:S(2)}) collective-permute-start(bf16[192,512]{1,0:T(8,128)(2,1)} %get-tuple-element.141), channel_id=1, source_target_pairs={{0,132},{1,133},{2,134},{3,135},{4,128},{5,129},{6,130},{7,131},{8... | collective-permute-start | bytes 589832 | tf_op jit(solution)/shard_map/ppermute | solution.py:16
  102.5 1.3 conditional.3
  102.5 1.3 collective-permute-start.16
  103.8 0.8 collective-permute-done.48.a_ref
  104.6 2.3 %collective-permute-done.49.b_ref = bf16[192,512]{1,0:T(8,128)(2,1)S(1)} collective-permute-done((bf16[192,512]{1,0:T(8,128)(2,1)}, bf16[192,512]{1,0:T(8,128)(2,1)S(1)}, u32[]{:S(2)}, u32[]{:S(2)}) %collective-permute-start.49) | collective-permute-done | bytes 196640 | tf_op jit(solution)/shard_map/ppermute | solution.py:16
  107.0 4.6 %collective-permute-done.50.c_ref = bf16[192,512]{1,0:T(8,128)(2,1)S(1)} collective-permute-done((bf16[192,512]{1,0:T(8,128)(2,1)}, bf16[192,512]{1,0:T(8,128)(2,1)S(1)}, u32[]{:S(2)}, u32[]{:S(2)}) %collective-permute-start.50) | collective-permute-done | bytes 196640 | tf_op jit(solution)/shard_map/ppermute | solution.py:16
  111.6 0.7 copy-done.19
  112.3 2.1 %third_sum.1 = (f32[32,512]{1,0:T(8,128)}, f32[32,512]{1,0:T(8,128)}, bf16[96,512]{1,0:T(8,128)(2,1)}, bf16[96,512]{1,0:T(8,128)(2,1)}, bf16[96,512]{1,0:T(8,128)(2,1)}) custom-call(s32[4]{0:T(128)} %pad_add_fusion.at_ref, f32[128,512]{1,0:T(8,128)} %get-tuple-element.143.large_ref, f32[32,512]{1,0:T(8,128)} %get-tuple-element.144.terms_ref, ...), custom_call_target="tpu_custom_call" | custom-call | flops 800000000 | bytes 2000000 | tf_op jit(solution)/shard_map/third_sum/pallas_call | solution.py:254
  114.3 0.1 collective-permute-start.52
  114.4 3.5 %collective-permute-start.53 = (bf16[96,512]{1,0:T(8,128)(2,1)}, bf16[96,512]{1,0:T(8,128)(2,1)S(1)}, u32[]{:S(2)}, u32[]{:S(2)}) collective-permute-start(bf16[96,512]{1,0:T(8,128)(2,1)} %get-tuple-element.152), channel_id=1, source_target_pairs={{0,48},{1,49},{2,50},{3,51},{4,52},{5,53},{6,54},{7,55},{8,56},{9,... | collective-permute-start | bytes 294920 | tf_op jit(solution)/shard_map/ppermute | solution.py:16
  117.9 0.1 collective-permute-done.51.a_ref
  118.0 1.3 collective-permute-done.52.b_ref
  119.4 2.7 %collective-permute-done.53.c_ref = bf16[96,512]{1,0:T(8,128)(2,1)S(1)} collective-permute-done((bf16[96,512]{1,0:T(8,128)(2,1)}, bf16[96,512]{1,0:T(8,128)(2,1)S(1)}, u32[]{:S(2)}, u32[]{:S(2)}) %collective-permute-start.53) | collective-permute-done | bytes 98336 | tf_op jit(solution)/shard_map/ppermute | solution.py:16
  122.0 0.8 copy-done.8
  122.9 0.8 copy-done.9
  123.7 4.7 %collective-permute-start.54 = (f32[48,512]{1,0:T(8,128)S(1)}, f32[48,512]{1,0:T(8,128)S(1)}, u32[]{:S(2)}, u32[]{:S(2)}) collective-permute-start(f32[48,512]{1,0:T(8,128)S(1)} %get-tuple-element.155), channel_id=1, source_target_pairs={{0,96},{1,97},{2,98},{3,99},{4,100},{5,101},{6,102},{7,103},{8,104... | collective-permute-start | bytes 294920 | tf_op jit(solution)/shard_map/ppermute | solution.py:16
  128.5 0.9 convert_add_fusion.1
  129.4 1.1 collective-permute-done.54.got_ref
  130.5 0.6 last_sum.1
  131.1 4.1 %collective-permute-start.55 = (f32[32,512]{1,0:T(8,128)S(1)}, f32[32,512]{1,0:T(8,128)S(1)}, u32[]{:S(2)}, u32[]{:S(2)}) collective-permute-start(f32[32,512]{1,0:T(8,128)S(1)} %get-tuple-element.158.half_ref), channel_id=1, source_target_pairs={{0,8},{1,9},{2,10},{3,11},{4,12},{5,13},{6,14},{7,15},{8,0},{9,1},... | collective-permute-start | bytes 196616 | tf_op jit(solution)/shard_map/ppermute | solution.py:16
  135.3 0.9 fusion.12
  136.2 1.2 split.1
  (64 shorter events, 0.4 us)
Async XLA Ops:
  0.6 15.1 %copy-start = (bf16[2048,512]{1,0:T(8,128)(2,1)S(1)}, bf16[2048,512]{1,0:T(8,128)(2,1)}, u32[]{:S(2)}) copy-start(bf16[2048,512]{1,0:T(8,128)(2,1)} %param.49) | copy-start | bytes 6291460
  3.7 1.3 collective-permute-start
  5.0 13.8 %collective-permute-start.34 = (bf16[16,3,512]{2,1,0:T(4,128)(2,1)}, bf16[16,3,512]{2,1,0:T(4,128)(2,1)S(1)}, u32[]{:S(2)}, u32[]{:S(2)}) collective-permute-start(bf16[16,3,512]{2,1,0:T(4,128)(2,1)} %get-tuple-element.175), channel_id=1, source_target_pairs={{0,8},{8,16},{16,24},{24,32},{32,40},{40,48},{48,56},{56,64},{64,7... | collective-permute-start | bytes 147464 | tf_op jit(solution)/shard_map/ppermute | solution.py:20
  7.2 11.6 %collective-permute-start.33 = (bf16[16,3,512]{2,1,0:T(4,128)(2,1)}, bf16[16,3,512]{2,1,0:T(4,128)(2,1)S(1)}, u32[]{:S(2)}, u32[]{:S(2)}) collective-permute-start(bf16[16,3,512]{2,1,0:T(4,128)(2,1)} %get-tuple-element.175), channel_id=1, source_target_pairs={{8,0},{16,8},{24,16},{32,24},{40,32},{48,40},{56,48},{64,56},{72,6... | collective-permute-start | bytes 147464 | tf_op jit(solution)/shard_map/ppermute | solution.py:24
  7.2 13.6 %collective-permute-start.32 = (bf16[16,3,512]{2,1,0:T(4,128)(2,1)S(1)}, bf16[16,3,512]{2,1,0:T(4,128)(2,1)S(1)}, u32[]{:S(2)}, u32[]{:S(2)}) collective-permute-start(bf16[16,3,512]{2,1,0:T(4,128)(2,1)S(1)} %get-tuple-element.170), channel_id=1, source_target_pairs={{0,1},{1,2},{2,3},{3,4},{4,5},{5,6},{6,7},{8,9},{9,10},{10,11},{11... | collective-permute-start | bytes 147464 | tf_op jit(solution)/shard_map/ppermute | solution.py:28
  11.9 8.9 %collective-permute-start.35 = (bf16[16,3,512]{2,1,0:T(4,128)(2,1)S(1)}, bf16[16,3,512]{2,1,0:T(4,128)(2,1)S(1)}, u32[]{:S(2)}, u32[]{:S(2)}) collective-permute-start(bf16[16,3,512]{2,1,0:T(4,128)(2,1)S(1)} %get-tuple-element.169), channel_id=1, source_target_pairs={{1,0},{2,1},{3,2},{4,3},{5,4},{6,5},{7,6},{9,8},{10,9},{11,10},{12... | collective-permute-start | bytes 147464 | tf_op jit(solution)/shard_map/ppermute | solution.py:32
  15.7 2.1 %copy-start.14 = (bf16[256,512]{1,0:T(8,128)(2,1)}, bf16[256,512]{1,0:T(8,128)(2,1)S(1)}, u32[]{:S(2)}) copy-start(bf16[256,512]{1,0:T(8,128)(2,1)S(1)} %bitcast_multiply_fusion.d_out_ref) | copy-start | bytes 786436
  17.8 3.0 %copy-start.12 = (bf16[16,16,512]{2,1,0:T(8,128)(2,1)S(1)}, bf16[16,16,512]{2,1,0:T(8,128)(2,1)}, u32[]{:S(2)}) copy-start(bf16[16,16,512]{2,1,0:T(8,128)(2,1)} %param.41) | copy-start | bytes 786436
  20.9 6.7 %collective-permute-start.37 = (bf16[3,22,512]{2,1,0:T(8,128)(2,1)S(1)}, bf16[3,22,512]{2,1,0:T(8,128)(2,1)S(1)}, u32[]{:S(2)}, u32[]{:S(2)}) collective-permute-start(bf16[3,22,512]{2,1,0:T(8,128)(2,1)S(1)} %get-tuple-element.168), channel_id=1, source_target_pairs={{8,0},{16,8},{24,16},{32,24},{40,32},{48,40},{56,48},{64,56},{72,6... | collective-permute-start | bytes 202760 | tf_op jit(solution)/shard_map/ppermute | solution.py:24
  26.7 1.4 %collective-permute-start.36 = (bf16[3,22,512]{2,1,0:T(8,128)(2,1)S(1)}, bf16[3,22,512]{2,1,0:T(8,128)(2,1)S(1)}, u32[]{:S(2)}, u32[]{:S(2)}) collective-permute-start(bf16[3,22,512]{2,1,0:T(8,128)(2,1)S(1)} %get-tuple-element.167), channel_id=1, source_target_pairs={{0,8},{8,16},{16,24},{24,32},{32,40},{40,48},{48,56},{56,64},{64,7... | collective-permute-start | bytes 202760 | tf_op jit(solution)/shard_map/ppermute | solution.py:20
  29.3 18.7 %copy-start.6 = (f32[49,512]{1,0:T(8,128)S(1)}, f32[49,512]{1,0:T(8,128)}, u32[]{:S(2)}) copy-start(f32[49,512]{1,0:T(8,128)} %kern_ref.3) | copy-start | bytes 301060
  43.2 9.7 %collective-permute-start.38 = (bf16[2112,512]{1,0:T(8,128)(2,1)}, bf16[2112,512]{1,0:T(8,128)(2,1)S(1)}, u32[]{:S(2)}, u32[]{:S(2)}) collective-permute-start(bf16[2112,512]{1,0:T(8,128)(2,1)} %get-tuple-element.119), channel_id=1, source_target_pairs={{0,8},{1,9},{2,10},{3,11},{4,12},{5,13},{6,14},{7,15},{8,0},{9,1},... | collective-permute-start | bytes 6488072 | tf_op jit(solution)/shard_map/ppermute | solution.py:16
  48.0 1.0 copy-start.10
  49.0 5.7 %copy-start.1 = (bf16[3,512,512]{2,1,0:T(8,128)(2,1)S(1)}, bf16[3,512,512]{2,1,0:T(8,128)(2,1)}, u32[]{:S(2)}) copy-start(bf16[3,512,512]{2,1,0:T(8,128)(2,1)} %get-tuple-element.125.keep_ref) | copy-start | bytes 4718596
  49.0 5.7 %copy-start.2 = (f32[512,512]{1,0:T(8,128)S(1)}, f32[512,512]{1,0:T(8,128)}, u32[]{:S(2)}) copy-start(f32[512,512]{1,0:T(8,128)} %get-tuple-element.124.mine_ref) | copy-start | bytes 3145732
  49.1 5.7 %copy-start.3 = (f32[32,512]{1,0:T(8,128)S(1)}, f32[32,512]{1,0:T(8,128)}, u32[]{:S(2)}) copy-start(f32[32,512]{1,0:T(8,128)} %get-tuple-element.127.half_ref) | copy-start | bytes 196612
  52.9 6.7 %collective-permute-start.40 = (bf16[3,32,512]{2,1,0:T(8,128)(2,1)S(1)}, bf16[3,32,512]{2,1,0:T(8,128)(2,1)S(1)}, u32[]{:S(2)}, u32[]{:S(2)}) collective-permute-start(bf16[3,32,512]{2,1,0:T(8,128)(2,1)S(1)} %get-tuple-element.123), channel_id=1, source_target_pairs={{8,0},{16,8},{24,16},{32,24},{40,32},{48,40},{56,48},{64,56},{72,6... | collective-permute-start | bytes 294920 | tf_op jit(solution)/shard_map/ppermute | solution.py:24
  53.0 6.7 %collective-permute-start.39 = (bf16[3,32,512]{2,1,0:T(8,128)(2,1)S(1)}, bf16[3,32,512]{2,1,0:T(8,128)(2,1)S(1)}, u32[]{:S(2)}, u32[]{:S(2)}) collective-permute-start(bf16[3,32,512]{2,1,0:T(8,128)(2,1)S(1)} %get-tuple-element.122), channel_id=1, source_target_pairs={{0,8},{8,16},{16,24},{24,32},{32,40},{40,48},{48,56},{56,64},{64,7... | collective-permute-start | bytes 294920 | tf_op jit(solution)/shard_map/ppermute | solution.py:20
  55.8 4.9 %copy-start.5 = (f32[512,512]{1,0:T(8,128)}, f32[512,512]{1,0:T(8,128)S(1)}, u32[]{:S(2)}) copy-start(f32[512,512]{1,0:T(8,128)S(1)} %get-tuple-element.134.own_ref) | copy-start | bytes 3145732
  55.8 4.9 %copy-start.7 = (f32[32,512]{1,0:T(8,128)}, f32[32,512]{1,0:T(8,128)S(1)}, u32[]{:S(2)}) copy-start(f32[32,512]{1,0:T(8,128)S(1)} %get-tuple-element.135.terms_ref) | copy-start | bytes 196612
  55.8 39.5 %collective-permute-start.45 = (bf16[576,512]{1,0:T(8,128)(2,1)}, bf16[576,512]{1,0:T(8,128)(2,1)}, u32[]{:S(2)}, u32[]{:S(2)}) collective-permute-start(bf16[576,512]{1,0:T(8,128)(2,1)} %get-tuple-element.128), channel_id=1, source_target_pairs={{0,1},{1,0},{2,3},{3,2},{4,5},{5,4},{6,7},{7,6},{8,9},{9,8},{10,11... | collective-permute-start | bytes 1769480 | tf_op jit(solution)/shard_map/ppermute | solution.py:16
  55.8 39.5 %collective-permute-start.46 = (bf16[576,512]{1,0:T(8,128)(2,1)S(1)}, bf16[576,512]{1,0:T(8,128)(2,1)}, u32[]{:S(2)}, u32[]{:S(2)}) collective-permute-start(bf16[576,512]{1,0:T(8,128)(2,1)S(1)} %get-tuple-element.129), channel_id=1, source_target_pairs={{0,2},{1,3},{2,0},{3,1},{4,6},{5,7},{6,4},{7,5},{8,10},{9,11},{10,... | collective-permute-start | bytes 1769480 | tf_op jit(solution)/shard_map/ppermute | solution.py:16
  55.8 39.5 %collective-permute-start.47 = (bf16[576,512]{1,0:T(8,128)(2,1)S(1)}, bf16[576,512]{1,0:T(8,128)(2,1)}, u32[]{:S(2)}, u32[]{:S(2)}) collective-permute-start(bf16[576,512]{1,0:T(8,128)(2,1)S(1)} %get-tuple-element.130), channel_id=1, source_target_pairs={{0,3},{1,2},{2,1},{3,0},{4,7},{5,6},{6,5},{7,4},{8,11},{9,10},{10,... | collective-permute-start | bytes 1769480 | tf_op jit(solution)/shard_map/ppermute | solution.py:16
  61.2 1.3 collective-permute-start.42
  61.9 10.6 %collective-permute-start.41 = (bf16[16,3,512]{2,1,0:T(4,128)(2,1)S(1)}, bf16[16,3,512]{2,1,0:T(4,128)(2,1)S(1)}, u32[]{:S(2)}, u32[]{:S(2)}) collective-permute-start(bf16[16,3,512]{2,1,0:T(4,128)(2,1)S(1)} %get-tuple-element.171), channel_id=1, source_target_pairs={{7,15},{15,23},{23,31},{31,39},{39,47},{47,55},{55,63},{63,71},{71... | collective-permute-start | bytes 147464 | tf_op jit(solution)/shard_map/ppermute | solution.py:37
  62.5 24.2 %collective-permute-start.43 = (bf16[16,3,512]{2,1,0:T(4,128)(2,1)S(1)}, bf16[16,3,512]{2,1,0:T(4,128)(2,1)S(1)}, u32[]{:S(2)}, u32[]{:S(2)}) collective-permute-start(bf16[16,3,512]{2,1,0:T(4,128)(2,1)S(1)} %get-tuple-element.166), channel_id=1, source_target_pairs={{0,1},{1,2},{2,3},{3,4},{4,5},{5,6},{6,7},{8,9},{9,10},{10,11},{11... | collective-permute-start | bytes 147464 | tf_op jit(solution)/shard_map/ppermute | solution.py:28
  72.5 22.8 %collective-permute-start.44 = (bf16[16,3,512]{2,1,0:T(4,128)(2,1)S(1)}, bf16[16,3,512]{2,1,0:T(4,128)(2,1)S(1)}, u32[]{:S(2)}, u32[]{:S(2)}) collective-permute-start(bf16[16,3,512]{2,1,0:T(4,128)(2,1)S(1)} %get-tuple-element.164), channel_id=1, source_target_pairs={{1,0},{2,1},{3,2},{4,3},{5,4},{6,5},{7,6},{9,8},{10,9},{11,10},{12... | collective-permute-start | bytes 147464 | tf_op jit(solution)/shard_map/ppermute | solution.py:32
  95.3 0.6 copy-start.15
  98.7 6.0 %collective-permute-start.48 = (bf16[192,512]{1,0:T(8,128)(2,1)}, bf16[192,512]{1,0:T(8,128)(2,1)S(1)}, u32[]{:S(2)}, u32[]{:S(2)}) collective-permute-start(bf16[192,512]{1,0:T(8,128)(2,1)} %get-tuple-element.139), channel_id=1, source_target_pairs={{0,128},{1,129},{2,130},{3,131},{4,132},{5,133},{6,134},{7,135},{8... | collective-permute-start | bytes 589832 | tf_op jit(solution)/shard_map/ppermute | solution.py:16
  98.7 8.3 %collective-permute-start.49 = (bf16[192,512]{1,0:T(8,128)(2,1)}, bf16[192,512]{1,0:T(8,128)(2,1)S(1)}, u32[]{:S(2)}, u32[]{:S(2)}) collective-permute-start(bf16[192,512]{1,0:T(8,128)(2,1)} %get-tuple-element.140), channel_id=1, source_target_pairs={{0,4},{1,5},{2,6},{3,7},{4,0},{5,1},{6,2},{7,3},{8,12},{9,13},{10,... | collective-permute-start | bytes 589832 | tf_op jit(solution)/shard_map/ppermute | solution.py:16
  98.7 12.9 %collective-permute-start.50 = (bf16[192,512]{1,0:T(8,128)(2,1)}, bf16[192,512]{1,0:T(8,128)(2,1)S(1)}, u32[]{:S(2)}, u32[]{:S(2)}) collective-permute-start(bf16[192,512]{1,0:T(8,128)(2,1)} %get-tuple-element.141), channel_id=1, source_target_pairs={{0,132},{1,133},{2,134},{3,135},{4,128},{5,129},{6,130},{7,131},{8... | collective-permute-start | bytes 589832 | tf_op jit(solution)/shard_map/ppermute | solution.py:16
  102.5 1.3 collective-permute-start.16
  104.6 6.9 %copy-start.17 = (bf16[192,512]{1,0:T(8,128)(2,1)}, bf16[192,512]{1,0:T(8,128)(2,1)S(1)}, u32[]{:S(2)}) copy-start(bf16[192,512]{1,0:T(8,128)(2,1)S(1)} %collective-permute-done.48.a_ref) | copy-start | bytes 589828
  107.0 4.6 %copy-start.18 = (bf16[192,512]{1,0:T(8,128)(2,1)}, bf16[192,512]{1,0:T(8,128)(2,1)S(1)}, u32[]{:S(2)}) copy-start(bf16[192,512]{1,0:T(8,128)(2,1)S(1)} %collective-permute-done.49.b_ref) | copy-start | bytes 589828
  111.6 0.7 copy-start.19
  114.3 3.7 %collective-permute-start.51 = (bf16[96,512]{1,0:T(8,128)(2,1)}, bf16[96,512]{1,0:T(8,128)(2,1)S(1)}, u32[]{:S(2)}, u32[]{:S(2)}) collective-permute-start(bf16[96,512]{1,0:T(8,128)(2,1)} %get-tuple-element.150), channel_id=1, source_target_pairs={{0,16},{1,17},{2,18},{3,19},{4,20},{5,21},{6,22},{7,23},{8,24},{9,... | collective-permute-start | bytes 294920 | tf_op jit(solution)/shard_map/ppermute | solution.py:16
  114.3 5.0 %collective-permute-start.52 = (bf16[96,512]{1,0:T(8,128)(2,1)}, bf16[96,512]{1,0:T(8,128)(2,1)S(1)}, u32[]{:S(2)}, u32[]{:S(2)}) collective-permute-start(bf16[96,512]{1,0:T(8,128)(2,1)} %get-tuple-element.151), channel_id=1, source_target_pairs={{0,32},{1,33},{2,34},{3,35},{4,36},{5,37},{6,38},{7,39},{8,40},{9,... | collective-permute-start | bytes 294920 | tf_op jit(solution)/shard_map/ppermute | solution.py:16
  114.4 7.6 %collective-permute-start.53 = (bf16[96,512]{1,0:T(8,128)(2,1)}, bf16[96,512]{1,0:T(8,128)(2,1)S(1)}, u32[]{:S(2)}, u32[]{:S(2)}) collective-permute-start(bf16[96,512]{1,0:T(8,128)(2,1)} %get-tuple-element.152), channel_id=1, source_target_pairs={{0,48},{1,49},{2,50},{3,51},{4,52},{5,53},{6,54},{7,55},{8,56},{9,... | collective-permute-start | bytes 294920 | tf_op jit(solution)/shard_map/ppermute | solution.py:16
  122.0 0.8 copy-start.8
  122.9 0.8 copy-start.9
  123.7 4.8 %copy-start.16 = (bf16[16,3,512]{2,1,0:T(4,128)(2,1)S(1)}, bf16[16,3,512]{2,1,0:T(4,128)(2,1)}, u32[]{:S(2)}) copy-start(bf16[16,3,512]{2,1,0:T(4,128)(2,1)} %copy-done.15) | copy-start | bytes 147460
  123.7 6.8 %collective-permute-start.54 = (f32[48,512]{1,0:T(8,128)S(1)}, f32[48,512]{1,0:T(8,128)S(1)}, u32[]{:S(2)}, u32[]{:S(2)}) collective-permute-start(f32[48,512]{1,0:T(8,128)S(1)} %get-tuple-element.155), channel_id=1, source_target_pairs={{0,96},{1,97},{2,98},{3,99},{4,100},{5,101},{6,102},{7,103},{8,104... | collective-permute-start | bytes 294920 | tf_op jit(solution)/shard_map/ppermute | solution.py:16
  130.5 4.8 %copy-start.11 = (f32[16,22,512]{2,1,0:T(8,128)S(1)}, f32[16,22,512]{2,1,0:T(8,128)}, u32[]{:S(2)}) copy-start(f32[16,22,512]{2,1,0:T(8,128)} %get-tuple-element.163) | copy-start | bytes 2162692
  130.5 4.8 %copy-start.13 = (bf16[16,16,512]{2,1,0:T(8,128)(2,1)S(1)}, bf16[16,16,512]{2,1,0:T(8,128)(2,1)}, u32[]{:S(2)}) copy-start(bf16[16,16,512]{2,1,0:T(8,128)(2,1)} %param.42) | copy-start | bytes 786436
  130.5 5.7 %copy-start.4 = (s32[4]{0:T(128)S(1)}, s32[4]{0:T(128)}, u32[]{:S(2)}) copy-start(s32[4]{0:T(128)} %pad_add_fusion.at_ref) | copy-start | bytes 52
  131.1 5.0 %collective-permute-start.55 = (f32[32,512]{1,0:T(8,128)S(1)}, f32[32,512]{1,0:T(8,128)S(1)}, u32[]{:S(2)}, u32[]{:S(2)}) collective-permute-start(f32[32,512]{1,0:T(8,128)S(1)} %get-tuple-element.158.half_ref), channel_id=1, source_target_pairs={{0,8},{1,9},{2,10},{3,11},{4,12},{5,13},{6,14},{7,15},{8,0},{9,1},... | collective-permute-start | bytes 196616 | tf_op jit(solution)/shard_map/ppermute | solution.py:16
